TPU v7x, 512 devices: a whole 4x4x16 slice. The times are simulated.
512 devices in a mesh: ctx: 128 (over z, y_lo, x), ch: 4 (over y_hi, core).
Axes of the slice: x: 4, y: 4 (y_hi: 2, y_lo: 2; y = y_hi * 2 + y_lo), z: 16, core: 2. Of those that a mesh axis runs over, the one named last changes fastest.
Arguments:
- tokens: bfloat16 [16384, 4096], P('ctx'), may hold values from -1000 to 1000, as said below
- norm_gain: float32 [4096], replicated, may hold values from 0.1 to 1.9
- in_proj: bfloat16 [4096, 3, 2048], P('ctx', None, 'ch'), may hold values from -0.09375 to 0.09375
- short_taps: float32 [3, 3, 2048], P(None, None, 'ch'), may hold values from -3 to 3
- decay: float32 [16, 2048], P(None, 'ch'), may hold values from 0 to 1, as said below
- residue: float32 [16, 2048], P(None, 'ch'), may hold values from -1.5 to 1.5
- skip: float32 [2048], P('ch'), may hold values from -4 to 4
Outputs:
- mixed: bfloat16 [16384, 2048], P('ctx', 'ch')
Inputs may be any that keep to these rules, and one draw needn't show every extreme that they name: `tokens`: every entry is finite. `decay`: every rate is positive.
All inputs are finite; a program needn't handle non-finite values.
Results may differ from a plain program's by a relative error of at most 0.01295.
Values may be sent and summed in bfloat16 or wider, within the bound.
A program may use at most 128 MiB of HBM per device.

v0:
```python
import math

import jax
import jax.numpy as jnp
from jax import lax
from jax.sharding import PartitionSpec as P


def passed_along(value, axis, steps):
    count = lax.axis_size(axis)
    initial, last = (max(0, -steps), min(count, count - steps))
    return lax.ppermute(value, axis, [(source, source + steps) for source in range(initial, last)])


def shortened(array):
    return jax.tree.map(lambda a: a.astype(jnp.bfloat16) if a.dtype == jnp.float32 else a, array)


def phase_table(left_index, right_index, period):
    product = left_index[:, None] * right_index[None, :] % period
    product = jnp.where(product > period // 2, product - period, product)
    return product.astype(jnp.float32) * (2.0 * math.pi / period)


def contract_rows(matrix, values):
    return jnp.einsum("sr,krc->ksc", matrix, values, precision=lax.Precision.HIGHEST)


def first_forward(blocks, r_index, total_len):
    count = blocks.shape[0]
    freq_index = jnp.arange(2 * count, dtype=jnp.int32)
    phases = phase_table(freq_index, jnp.arange(count, dtype=jnp.int32), 2 * count)
    flat = blocks.reshape(count, -1)
    out_shape = (2 * count,) + blocks.shape[1:]
    real_part = jnp.dot(jnp.cos(phases), flat, precision=lax.Precision.HIGHEST).reshape(out_shape)
    imag_part = -jnp.dot(jnp.sin(phases), flat, precision=lax.Precision.HIGHEST).reshape(out_shape)
    twist = phase_table(freq_index, r_index, total_len)
    cosine = jnp.cos(twist)[:, :, None]
    sine = jnp.sin(twist)[:, :, None]
    return (real_part * cosine + imag_part * sine, imag_part * cosine - real_part * sine)


def second_forward(real_part, imag_part):
    length = real_part.shape[1]
    steps_index = jnp.arange(length, dtype=jnp.int32)
    phases = phase_table(steps_index, steps_index, length)
    cosine = jnp.cos(phases)
    sine = jnp.sin(phases)
    out_real = contract_rows(cosine, real_part) + contract_rows(sine, imag_part)
    out_imag = contract_rows(cosine, imag_part) - contract_rows(sine, real_part)
    return (out_real, out_imag)


def first_inverse(real_part, imag_part, freq_index, total_len):
    length = real_part.shape[1]
    steps_index = jnp.arange(length, dtype=jnp.int32)
    phases = phase_table(steps_index, steps_index, length)
    cosine = jnp.cos(phases)
    sine = jnp.sin(phases)
    mid_real = contract_rows(cosine, real_part) - contract_rows(sine, imag_part)
    mid_imag = contract_rows(cosine, imag_part) + contract_rows(sine, real_part)
    twist = phase_table(freq_index, steps_index, total_len)
    tw_cos = jnp.cos(twist)[:, :, None]
    tw_sin = jnp.sin(twist)[:, :, None]
    return (mid_real * tw_cos - mid_imag * tw_sin, mid_imag * tw_cos + mid_real * tw_sin)


def second_inverse(real_part, imag_part, total_len):
    doubled = real_part.shape[0]
    count = doubled // 2
    phases = phase_table(
        jnp.arange(count, dtype=jnp.int32), jnp.arange(doubled, dtype=jnp.int32), doubled
    )
    flat_real = real_part.reshape(doubled, -1)
    flat_imag = imag_part.reshape(doubled, -1)
    result = jnp.dot(jnp.cos(phases), flat_real, precision=lax.Precision.HIGHEST)
    result = result - jnp.dot(jnp.sin(phases), flat_imag, precision=lax.Precision.HIGHEST)
    return (result * (1.0 / total_len)).reshape((count,) + real_part.shape[1:])


def spectrum(freq_index, decay_cols, residue_cols, length, count, seq_len, total_len):
    freq = freq_index[:, None] + 2 * count * jnp.arange(length, dtype=jnp.int32)[None, :]
    symmetric = jnp.where(freq > total_len // 2, freq - total_len, freq)
    half_phase = symmetric.astype(jnp.float32) * (math.pi / total_len)
    half_sq = (jnp.sin(half_phase) ** 2)[:, :, None]
    full_sin = jnp.sin(2.0 * half_phase)[:, :, None]
    parity = (1 - 2 * (freq % 2)).astype(jnp.float32)[:, :, None]
    shape_out = (freq_index.shape[0], length, decay_cols.shape[1])

    def add_mode(mode, carried):
        acc_real, acc_imag = carried
        rate = decay_cols[mode]
        amplitude = residue_cols[mode] * jnp.sqrt(2.0 * rate)
        ratio = jnp.exp(-rate)
        gap_term = -jnp.expm1(-rate)
        tail_term = jnp.exp(-rate * seq_len)
        along = gap_term + 2.0 * ratio * half_sq
        across = ratio * full_sin
        denom = gap_term * gap_term + 4.0 * ratio * half_sq
        numer = amplitude * (1.0 - tail_term * parity) / denom
        return (acc_real + numer * along, acc_imag - numer * across)

    zeros_block = jnp.zeros(shape_out, jnp.float32)
    return lax.fori_loop(0, decay_cols.shape[0], add_mode, (zeros_block, zeros_block))


def local(tokens, norm_gain, in_proj, short_taps, decay, residue, skip):
    tok_rows = tokens.shape[0]
    channels = in_proj.shape[2]
    devices = lax.axis_size("ctx")
    position = lax.axis_index("ctx")
    as_float = tokens.astype(jnp.float32)
    mean_square = jnp.mean(as_float * as_float, axis=1, keepdims=True)
    normed = (as_float * lax.rsqrt(mean_square + 1e-06) * norm_gain).astype(jnp.bfloat16)
    weight_piece = lax.all_gather(in_proj, "ctx", axis=0, tiled=True)
    piece_rows = weight_piece.shape[0]
    flat_piece = weight_piece.reshape(piece_rows, 3 * channels)
    projected = jnp.dot(normed, flat_piece, preferred_element_type=jnp.float32)
    proj = projected.astype(jnp.bfloat16).reshape(tok_rows, 3, channels)
    tap_count = short_taps.shape[0]
    rim_rows = passed_along(proj[tok_rows - (tap_count - 1) :], "ctx", 1)
    extended = jnp.concatenate([rim_rows, proj], axis=0)
    feats = jnp.zeros((tok_rows, 3, channels), jnp.float32)
    for shift_by in range(tap_count):
        window = extended[tap_count - 1 - shift_by : tap_count - 1 - shift_by + tok_rows].astype(
            jnp.float32
        )
        feats = feats + short_taps[shift_by] * window
    drive = feats[:, 1, :] * feats[:, 2, :]
    seq_len = tok_rows * devices
    total_len = 2 * seq_len
    group_rows = tok_rows // devices
    regrouped = drive.reshape(devices, group_rows, channels)
    arrived = lax.all_to_all(
        regrouped.astype(jnp.bfloat16), "ctx", split_axis=0, concat_axis=0, tiled=True
    ).astype(regrouped.dtype)
    r_index = position * group_rows + jnp.arange(group_rows, dtype=jnp.int32)
    front_real, front_imag = first_forward(arrived, r_index, total_len)
    middle = lax.all_to_all(
        jnp.stack([front_real, front_imag]).astype(jnp.bfloat16),
        "ctx",
        split_axis=1,
        concat_axis=2,
        tiled=True,
    ).astype(jnp.float32)
    spec_real, spec_imag = second_forward(middle[0], middle[1])
    freq_index = 2 * position + jnp.arange(2, dtype=jnp.int32)
    filt_real, filt_imag = spectrum(
        freq_index, decay, residue, tok_rows, devices, seq_len, total_len
    )
    prod_real = spec_real * filt_real - spec_imag * filt_imag
    prod_imag = spec_real * filt_imag + spec_imag * filt_real
    back_real, back_imag = first_inverse(prod_real, prod_imag, freq_index, total_len)
    returned = lax.all_to_all(
        shortened(jnp.stack([back_real, back_imag])), "ctx", split_axis=2, concat_axis=1, tiled=True
    )
    local_conv = second_inverse(returned[0], returned[1], total_len)
    conv = (
        lax.all_to_all(shortened(local_conv), "ctx", split_axis=0, concat_axis=1, tiled=True)
        .astype(local_conv.dtype)
        .reshape(tok_rows, channels)
    )
    return (feats[:, 0, :] * (conv + skip * drive)).astype(jnp.bfloat16)


def solution(mesh):
    placed = (
        P("ctx", None),
        P(),
        P("ctx", None, "ch"),
        P(None, None, "ch"),
        P(None, "ch"),
        P(None, "ch"),
        P("ch"),
    )
    return jax.shard_map(
        local, mesh=mesh, in_specs=placed, out_specs=P("ctx", "ch"), check_vma=False
    )
```

profile of v0, /device:TPU:8, one launch (start us, length us, event | category | flops | bytes accessed | tf_op | source)
XLA Modules:
  0.0 810.4 jit_solution(1913601212873430210)
XLA Ops:
  7.3 1.5 fusion.13
  8.8 611.6 %all-gather.2.cloned.1.call-done = bf16[4096,3,512]{2,0,1:T(8,128)(2,1)} async-done(((bf16[32,3,512]{2,0,1:T(8,128)(2,1)}), bf16[4096,3,512]{2,0,1:T(8,128)(2,1)}) %all-gather.2.cloned.1.call-update) | async-done | bytes 12582928 | tf_op jit(solution)/shard_map/all_gather | solution.py:115
  620.4 17.0 %copy.55 = bf16[4096,3,512]{0,2,1:T(8,128)(2,1)} copy(bf16[4096,3,512]{2,0,1:T(8,128)(2,1)} %all-gather.2.cloned.1.call-done) | data formatting | bytes 25165824 | tf_op jit(solution)/shard_map/all_gather | solution.py:115
  637.4 8.9 %convolution_convert_fusion = bf16[128,1536]{1,0:T(8,128)(2,1)S(1)} fusion(bf16[4096,1536]{0,1:T(8,128)(2,1)} %bitcast.120, bf16[128,4096]{1,0:T(8,128)(2,1)S(1)} %copy-done, f32[4096]{0:T(1024)S(1)} %copy-done.2, f32[128]{0:T(128)S(1)} %add_rsqrt_fusion), kind=kOutput, calls=%fused_computation.30 | convolution fusion | flops 1612906496 | bytes 14041600 | tf_op jit(solution)/shard_map/dot_general | solution.py:118
  646.6 3.3 collective-permute-start
  650.2 10.0 %collective-permute-done = bf16[2,3,512]{0,2,1:T(8,128)(2,1)S(1)} collective-permute-done((bf16[2,3,512]{0,2,1:T(8,128)(2,1)S(1)}, bf16[2,3,512]{0,2,1:T(8,128)(2,1)S(1)}, u32[]{:S(2)}, u32[]{:S(2)}) %collective-permute-start) | collective-permute-done | bytes 6176 | tf_op jit(solution)/shard_map/ppermute | solution.py:12
  660.2 1.1 multiply_add_fusion
  663.3 16.9 %all-to-all-start = ((bf16[128,2,256]{2,1,0:T(2,128)(2,1)}), bf16[128,2,256]{2,1,0:T(2,128)(2,1)S(1)}, u32[]{:S(2)}, u32[]{:S(2)}) async-start(bf16[128,2,256]{2,1,0:T(2,128)(2,1)} %reshape.468), calls=%async_computation | async-start | bytes 262144 | tf_op jit(solution)/shard_map/all_to_all | solution.py:134
  680.3 16.6 %all-to-all-done = bf16[128,2,256]{2,1,0:T(2,128)(2,1)S(1)} async-done(((bf16[128,2,256]{2,1,0:T(2,128)(2,1)}), bf16[128,2,256]{2,1,0:T(2,128)(2,1)S(1)}, u32[]{:S(2)}, u32[]{:S(2)}) %all-to-all-start) | async-done | bytes 131104 | tf_op jit(solution)/shard_map/all_to_all | solution.py:134
  697.0 0.8 convolution_negate_fusion
  697.9 0.9 fusion.25
  698.8 1.3 copy.59
  700.2 5.8 all-to-all-start.1
  705.9 22.7 %while.18 = (s32[]{:T(128)}, f32[2,128,512]{2,1,0:T(8,128)S(1)}, f32[2,128,512]{2,1,0:T(8,128)S(1)}, f32[16,512]{1,0:T(8,128)}, f32[16,512]{1,0:T(8,128)}, /*ind...) while((s32[]{:T(128)}, f32[2,128,512]{2,1,0:T(8,128)S(1)}, ...), condition=%wide.region_2.3_spmd.clone.clone.clone, body=%wide.region_1.2_spmd.clone.clone.clone.sunk | while | flops 1976067 | bytes 2139267 | solution.py:104
  706.1 0.8 sqrt_multiply_fusion.2
  707.5 0.8 sqrt_multiply_fusion.2
  708.9 0.8 sqrt_multiply_fusion.2
  710.3 0.8 sqrt_multiply_fusion.2
  711.7 0.8 sqrt_multiply_fusion.2
  713.2 0.8 sqrt_multiply_fusion.2
  714.6 0.8 sqrt_multiply_fusion.2
  716.0 0.8 sqrt_multiply_fusion.2
  717.4 0.8 sqrt_multiply_fusion.2
  732.7 0.8 fusion.61
  733.5 0.8 fusion.63
  734.3 0.8 convolution_add_fusion
  735.2 0.9 fusion.27
  736.7 40.1 %all_to_all.44 = bf16[2,2,128,512]{3,1,0,2:T(2,128)(2,1)S(1)} all-to-all(bf16[2,2,128,512]{3,1,0,2:T(2,128)(2,1)S(1)} %copy.65), channel_id=1, replica_groups=mesh['ctx'=128,'ch'=4] {'ctx'}, dimensions={2} | all-to-all | bytes 1048576 | tf_op jit(solution)/shard_map/all_to_all | solution.py:154
  777.3 0.8 fusion.47
  778.2 0.8 fusion.20
  779.7 22.6 %all_to_all.45 = bf16[128,2,256]{2,1,0:T(2,128)(2,1)S(1)} all-to-all(bf16[128,2,256]{2,1,0:T(2,128)(2,1)S(1)} %reshape.470), channel_id=1, replica_groups=mesh['ctx'=128,'ch'=4] {'ctx'}, dimensions={0} | all-to-all | bytes 262144 | tf_op jit(solution)/shard_map/all_to_all | solution.py:159
  802.7 0.8 copy.68
  (117 shorter events, 25.0 us)
Async XLA Ops:
  6.5 613.9 %all-gather.2.cloned.1.call-start = ((), (), s32[]{:S(2)}) async-start(), calls=%async_computation.4 | async-start | bytes 12681216 | tf_op jit(solution)/shard_map/all_gather | solution.py:115
  8.8 628.6 %copy-start = (bf16[128,4096]{1,0:T(8,128)(2,1)S(1)}, bf16[128,4096]{1,0:T(8,128)(2,1)}, u32[]{:S(2)}) copy-start(bf16[128,4096]{1,0:T(8,128)(2,1)} %param.9) | copy-start | bytes 3145732
  8.8 628.6 %copy-start.2 = (f32[4096]{0:T(1024)S(1)}, f32[4096]{0:T(1024)}, u32[]{:S(2)}) copy-start(f32[4096]{0:T(1024)} %param.10) | copy-start | bytes 49156
  637.4 12.5 %copy-start.1 = (f32[3,3,512]{2,1,0:T(4,128)S(1)}, f32[3,3,512]{2,1,0:T(4,128)}, u32[]{:S(2)}) copy-start(f32[3,3,512]{2,1,0:T(4,128)} %param.12) | copy-start | bytes 55300
  646.6 13.6 %collective-permute-start = (bf16[2,3,512]{0,2,1:T(8,128)(2,1)S(1)}, bf16[2,3,512]{0,2,1:T(8,128)(2,1)S(1)}, u32[]{:S(2)}, u32[]{:S(2)}) collective-permute-start(bf16[2,3,512]{0,2,1:T(8,128)(2,1)S(1)} %bitcast.130), channel_id=1, source_target_pairs={{0,4},{4,8},{8,12},{12,16},{16,20},{20,24},{24,28},{28,32},{32,36}... | collective-permute-start | bytes 18440 | tf_op jit(solution)/shard_map/ppermute | solution.py:12
  663.3 33.6 %all-to-all-start = ((bf16[128,2,256]{2,1,0:T(2,128)(2,1)}), bf16[128,2,256]{2,1,0:T(2,128)(2,1)S(1)}, u32[]{:S(2)}, u32[]{:S(2)}) async-start(bf16[128,2,256]{2,1,0:T(2,128)(2,1)} %reshape.468), calls=%async_computation | async-start | bytes 262144 | tf_op jit(solution)/shard_map/all_to_all | solution.py:134
  700.2 29.4 %all-to-all-start.1 = ((bf16[2,256,1,512]{3,0,2,1:T(2,128)(2,1)}), bf16[2,256,1,512]{3,0,2,1:T(2,128)(2,1)S(1)}, u32[]{:S(2)}, u32[]{:S(2)}) async-start(bf16[2,256,1,512]{3,0,2,1:T(2,128)(2,1)} %copy.59), calls=%async_computation.1 | async-start | bytes 1048576 | tf_op jit(solution)/shard_map/all_to_all | solution.py:139
  777.2 25.4 %copy-start.3 = (f32[512]{0:T(512)S(1)}, f32[512]{0:T(512)}, u32[]{:S(2)}) copy-start(f32[512]{0:T(512)} %param.15) | copy-start | bytes 6148
Sparse Core Ops, SparseCore 0:
  9.4 610.8 all-gather.1
where the time goes:
time: 814 us; the launch traced here: 810 us
  waiting for transfers between devices  639 us (79%)
  blocking collectives  62.8 us (8%)
  other arithmetic  26.5 us (3%)
  starting transfers between devices  26 us (3%)
  local copies, waits for them, and re-layouts  23.4 us (3%)
  matrix products  18.1 us (2%)
  between operations  13.7 us (2%)
    all_gather x1, waiting for transfers between devices, local(): weight_piece = lax.all_gather(in_proj, 'ctx', axis=0, tiled=True)  612 us
    all_to_all x1, blocking collectives, local(): lax.all_to_all(shortened(jnp.stack([back_real, back_imag])), 'ctx', split...  40.1 us
    all_to_all x1, blocking collectives, local(): lax.all_to_all(shortened(local_conv), 'ctx', split_axis=0, concat_axis=1,...  22.6 us
    all_gather x1, local copies, waits for them, and re-layouts, local(): weight_piece = lax.all_gather(in_proj, 'ctx', axis=0, tiled=True)  17 us
    all_to_all x1, starting transfers between devices, local(): lax.all_to_all(regrouped.astype(jnp.bfloat16), 'ctx', split_axis=0, conca...  16.9 us
    all_to_all x1, waiting for transfers between devices, local(): lax.all_to_all(regrouped.astype(jnp.bfloat16), 'ctx', split_axis=0, conca...  16.6 us
  transfers between devices with their start and end apart: 4, of which 4 were waited for; matrix products, arithmetic and copies ran while one was open for 3% of the time, Pallas kernels for 0%

commit v1 on v0

v1 whole, which is shorter than its diff:
```python
import functools

import jax
import jax.numpy as jnp
from jax import lax
from jax.experimental import pallas as pl
from jax.experimental.pallas import tpu as pltpu
from jax.sharding import PartitionSpec as P

MESH = pl.DeviceIdType.MESH
F32 = jnp.float32
BF16 = jnp.bfloat16

ROWS = 128
GROUP = 8
PIECE = 16
LANES = 128
HALF = 64
MODES = 16


def kernel(
    nz,
    tok_ref,
    gain_ref,
    w_ref,
    taps_ref,
    dec_ref,
    res_ref,
    skip_ref,
    o_ref,
    X,
    wa,
    slabs,
    wfull,
    proj,
    rim,
    drive_s,
    gate_s,
    lam_s,
    amp_s,
    l64_s,
    step_s,
    pow_s,
    zw_s,
    end_s,
    totals,
    obuf,
    outbuf,
    inbox,
    wa_send,
    wa_recv,
    tok_send,
    tok_recv,
    sib_recv,
    zp_send,
    zp_recv,
    zm_send,
    zm_recv,
    rim_sem,
    st_send,
    st_recv,
    out_send,
    out_recv,
):
    ctx = lax.axis_index("ctx")
    ch = lax.axis_index("ch")
    z = ctx // 8
    q = ctx % 8
    y_lo = q // 4
    x = q % 4
    y_hi = ch // 2
    core = ch % 2
    par = q % 2
    tile = q // 2
    base = z * 8

    def plane(yl, xx):
        return yl * 4 + xx

    x_up = (base + plane(y_lo, (x + 1) % 4), ch)
    x_dn = (base + plane(y_lo, (x + 3) % 4), ch)
    y = y_hi * 2 + y_lo
    y_a = (y + 1) % 4
    y_b = (y + 3) % 4
    y_up = (base + plane(y_a % 2, x), (y_a // 2) * 2 + core)
    y_dn = (base + plane(y_b % 2, x), (y_b // 2) * 2 + core)
    sib = (ctx, y_hi * 2 + (1 - core))
    z_up = (((z + 1) % nz) * 8 + q, ch)
    z_dn = (((z + nz - 1) % nz) * 8 + q, ch)
    y_far = (base + plane(1 - y_lo, x), (1 - y_hi) * 2 + core)

    barrier = pltpu.get_barrier_semaphore()

    def greet(dev):
        pl.semaphore_signal(barrier, inc=1, device_id=dev, device_id_type=MESH)

    @pl.loop(1, GROUP)
    def _(d):
        greet((base + (q + d) % 8, ch))

    @pl.loop(1, nz)
    def _(d):
        greet((((z + d) % nz) * 8 + q, ch))

    greet(y_far)
    greet(sib)

    lane = lax.broadcasted_iota(jnp.int32, (8, LANES), 1)
    left = lane < HALF
    sub = lax.broadcasted_iota(jnp.int32, (8, LANES), 0)

    def swap(v):
        return pltpu.roll(v, HALF, 1)

    def pick(v, lf):
        r = swap(v)
        even = jnp.where(lf, v, r)
        odd = jnp.where(lf, r, v)
        return jnp.where(par == 0, even, odd)

    j_own = plane(y_lo, x)
    j_up = plane(y_lo, (x + 1) % 4)
    j_dn = plane(y_lo, (x + 3) % 4)
    j_op = plane(y_lo, (x + 2) % 4)
    p_own = plane(1 - y_lo, x)
    p_up = plane(1 - y_lo, (x + 1) % 4)
    p_dn = plane(1 - y_lo, (x + 3) % 4)
    p_op = plane(1 - y_lo, (x + 2) % 4)

    def norm(half, piece):
        rows = pl.ds(pl.multiple_of(half * HALF + piece * PIECE, PIECE), PIECE)
        v = tok_ref[rows, :].astype(F32)
        ms = jnp.mean(v * v, axis=1, keepdims=True)
        X[j_own, rows, :] = (v * lax.rsqrt(ms + 1e-06) * gain_ref[...]).astype(BF16)

    norm(core, 0)
    norm(core, 2)
    pl.semaphore_wait(barrier, 7 + (nz - 1) + 2)

    sent = []

    def wa_copy(d):
        to = (q + d) % 8
        lanes = pl.ds(pl.multiple_of((to // 2) * LANES, LANES), LANES)
        return pltpu.make_async_remote_copy(
            src_ref=w_ref.at[:, :, lanes],
            dst_ref=wa.at[q],
            send_sem=wa_send.at[d],
            recv_sem=wa_recv.at[d],
            device_id=(base + to, ch),
            device_id_type=MESH,
        )

    @pl.loop(1, GROUP)
    def _(d):
        wa_copy(d).start()

    count = [0]

    def piece_ref(j, half, piece):
        return X.at[j, pl.ds(pl.multiple_of(half * HALF + piece * PIECE, PIECE), PIECE), :]

    def send(j, piece, dev):
        ref = piece_ref(j, core, piece)
        recv = (sib_recv if dev is sib else tok_recv).at[j * 4 + piece]
        copy = pltpu.make_async_remote_copy(
            src_ref=ref,
            dst_ref=ref,
            send_sem=tok_send.at[count[0]],
            recv_sem=recv,
            device_id=dev,
            device_id_type=MESH,
        )
        count[0] += 1
        copy.start()
        sent.append(copy)

    def arrive(j, piece):
        ref = piece_ref(j, core, piece)
        pltpu.make_async_remote_copy(
            src_ref=ref,
            dst_ref=ref,
            send_sem=tok_send.at[0],
            recv_sem=tok_recv.at[j * 4 + piece],
            device_id=sib,
            device_id_type=MESH,
        ).wait_recv()

    def arrive_sib(j, piece):
        ref = piece_ref(j, 1 - core, piece)
        pltpu.make_async_remote_copy(
            src_ref=ref,
            dst_ref=ref,
            send_sem=tok_send.at[0],
            recv_sem=sib_recv.at[j * 4 + piece],
            device_id=sib,
            device_id_type=MESH,
        ).wait_recv()

    send(j_own, 0, x_up)
    send(j_own, 2, x_dn)
    send(j_own, 0, y_up)
    send(j_own, 2, y_dn)
    norm(core, 1)
    norm(core, 3)
    send(j_own, 1, x_up)
    send(j_own, 3, x_dn)
    send(j_own, 1, y_up)
    send(j_own, 3, y_dn)
    send(j_own, 2, x_up)
    send(j_own, 0, x_dn)
    send(j_own, 3, x_up)
    send(j_own, 1, x_dn)

    wa[q] = w_ref[:, :, pl.ds(pl.multiple_of(tile * LANES, LANES), LANES)]

    @pl.loop(1, GROUP)
    def _(d):
        copy = wa_copy(d)
        pltpu.make_async_remote_copy(
            src_ref=wa.at[(q + 8 - d) % 8],
            dst_ref=wa.at[(q + 8 - d) % 8],
            send_sem=wa_send.at[d],
            recv_sem=wa_recv.at[d],
            device_id=sib,
            device_id_type=MESH,
        ).wait_recv()
        copy.wait_send()

    lane32 = lax.broadcasted_iota(jnp.int32, (32, LANES), 1)
    left32 = lane32 < HALF
    for g in range(GROUP):
        qk = jnp.where(left32, pick(wa[g, 0].astype(F32), left32), pick(wa[g, 1].astype(F32), left32))
        slabs[z, g * 32 : (g + 1) * 32, :] = qk.astype(BF16)
    for g in range(GROUP // 2):
        v = jnp.where(
            left32, pick(wa[g, 2].astype(F32), left32), pick(wa[g + 4, 2].astype(F32), left32)
        )
        slabs[z, 256 + g * 32 : 256 + (g + 1) * 32, :] = v.astype(BF16)

    def z_copy(step, up):
        s = (z + nz - step) % nz if up else (z + step) % nz
        sems, recvs = (zp_send, zp_recv) if up else (zm_send, zm_recv)
        return pltpu.make_async_remote_copy(
            src_ref=slabs.at[s],
            dst_ref=slabs.at[s],
            send_sem=sems.at[step],
            recv_sem=recvs.at[step],
            device_id=z_up if up else z_dn,
            device_id_type=MESH,
        )

    def z_arrived(step, up):
        s = (z + 2 * nz - step - 1) % nz if up else (z + step + 1) % nz
        sems, recvs = (zp_send, zp_recv) if up else (zm_send, zm_recv)
        pltpu.make_async_remote_copy(
            src_ref=slabs.at[s],
            dst_ref=slabs.at[s],
            send_sem=sems.at[step],
            recv_sem=recvs.at[step],
            device_id=z_up if up else z_dn,
            device_id_type=MESH,
        ).wait_recv()
        return s

    def unpack(s):
        at = pl.multiple_of(s * 256, 256)
        wfull[pl.ds(at, 256), 0:LANES] = slabs[s, 0:256, :]
        v = slabs[s, 256:384, :]
        wfull[pl.ds(at, 128), LANES:] = v
        wfull[pl.ds(at + 128, 128), LANES:] = swap(v.astype(F32)).astype(BF16)

    n_up = nz // 2
    n_dn = nz - 1 - n_up

    def z_start(step):
        for up, most in ((True, n_up), (False, n_dn)):
            if step < most:
                copy = z_copy(step, up)
                copy.start()
                sent.append(copy)

    def z_round(step):
        got = []
        for up, most in ((True, n_up), (False, n_dn)):
            if step < most:
                got.append(z_arrived(step, up))
        z_start(step + 1)
        return got

    z_start(0)

    for piece in range(4):
        norm(1 - core, piece)
    unpack(z)

    lanes_q = pl.ds(pl.multiple_of(tile * LANES, LANES), LANES)
    lane16 = lax.broadcasted_iota(jnp.int32, (MODES, LANES), 1)
    left16 = lane16 < HALF
    dec = pick(dec_ref[:, lanes_q], left16)
    res = pick(res_ref[:, lanes_q], left16)
    skp = pick(skip_ref[:, lanes_q] * jnp.ones((8, LANES), F32), left)
    amp = res * jnp.sqrt(2.0 * dec)
    lam = jnp.exp(-dec)
    l64 = jnp.exp(-dec * 64.0)
    ones8 = jnp.ones((8, LANES), F32)
    subf = sub.astype(F32)

    def constants():
        for s in range(MODES):
            d8 = dec[s : s + 1, :] * ones8
            lam_s[s] = lam[s : s + 1, :] * ones8
            amp_s[s] = amp[s : s + 1, :] * ones8
            l64_s[s] = l64[s : s + 1, :] * ones8
            for i, sh in enumerate((1, 2, 4)):
                step_s[i, s] = jnp.where(sub >= sh, jnp.exp(-d8 * (128.0 * sh)), 0.0)
            pow_s[s] = jnp.exp(-d8 * (128.0 * subf))
        dec_p = jnp.where(left, dec[0:8, :], dec[8:16, :])
        for s in range(nz):
            gap = (z - 1 - s).astype(F32)
            zw_s[s] = jnp.where(s < z, jnp.exp(-dec_p * (1024.0 * jnp.maximum(gap, 0.0))), 0.0)

    rounds = [
        [(j_dn, 0, (x_up, y_up)), (j_up, 2, (x_dn, y_dn)), (p_own, 0, ()), (p_own, 2, ())],
        [(j_dn, 1, (x_up, y_up)), (j_up, 3, (x_dn, y_dn)), (p_own, 1, ()), (p_own, 3, ())],
        [(j_dn, 2, (y_dn,)), (j_up, 0, (y_up,)), (p_dn, 0, ()), (p_up, 2, ())],
        [(j_dn, 3, (y_dn,)), (j_up, 1, (y_up,)), (p_dn, 1, ()), (p_up, 3, ())],
        [(j_op, 0, (y_up,)), (j_op, 2, (y_dn,)), (p_up, 0, ()), (p_dn, 2, ())],
        [(j_op, 1, (y_up,)), (j_op, 3, (y_dn,)), (p_up, 1, ()), (p_dn, 3, ())],
        [(p_op, 0, ()), (p_op, 2, ())],
        [(p_op, 1, ()), (p_op, 3, ())],
    ]

    left64 = lax.broadcasted_iota(jnp.int32, (HALF, LANES), 1) < HALF

    def project(j):
        acc = jnp.dot(X[j], wfull[...], preferred_element_type=F32)
        t0a, t0b = acc[0:HALF, 0:LANES], acc[HALF:, 0:LANES]
        t1a, t1b = acc[0:HALF, LANES:], acc[HALF:, LANES:]
        rows = pl.ds(pl.multiple_of(j * HALF, HALF), HALF)
        for i, v in enumerate(
            (
                jnp.where(left64, t0a, swap(t0b)),
                jnp.where(left64, swap(t0a), t0b),
                jnp.where(left64, t1a, swap(t1b)),
            )
        ):
            proj[i, rows, :] = v.astype(BF16).astype(F32)

    def project_when_here(j):
        for piece in range(4):
            arrive_sib(j, piece)
        project(j)

    for r, events in enumerate(rounds):
        got = z_round(r) if r < 7 else []
        for j, piece, onward in events:
            arrive(j, piece)
            for dev in onward:
                send(j, piece, dev)
            send(j, piece, sib)
        for s in got:
            unpack(s)
        if r == 0:
            constants()
        if r == 6:
            for s in z_round(7):
                unpack(s)
            project(j_own)
            project_when_here(p_own)
            project_when_here(j_dn)
            project_when_here(j_up)
    project_when_here(j_op)
    project_when_here(p_up)
    project_when_here(p_dn)
    project_when_here(p_op)

    rim_copy = pltpu.make_async_remote_copy(
        src_ref=proj.at[:, 504:512, :],
        dst_ref=rim,
        send_sem=rim_sem.at[0],
        recv_sem=rim_sem.at[1],
        device_id=z_up,
        device_id_type=MESH,
    )
    rim_copy.start()
    rim_copy.wait_recv()

    def at_step(i, r):
        return proj[i, pl.ds(r, 8, stride=HALF), :]

    def before(i, back):
        last = swap(at_step(i, HALF - back))
        edge = swap(rim[i, 8 - back : 9 - back, :] * ones8)
        edge = jnp.where(z == 0, 0.0, edge)
        shifted = jnp.where(sub == 0, edge, pltpu.roll(last, 1, 0))
        return jnp.where(left, shifted, last)

    taps = [
        [pick(taps_ref[3 * k + i : 3 * k + i + 1, lanes_q] * ones8, left) for i in range(3)]
        for k in range(3)
    ]

    def scan_one(r, carry):
        one, two, states = carry
        now = [at_step(i, r) for i in range(3)]
        feats = [taps[0][i] * now[i] + taps[1][i] * one[i] + taps[2][i] * two[i] for i in range(3)]
        drive = feats[1] * feats[2]
        drive_s[r] = drive
        gate_s[r] = feats[0]
        states = [lam_s[s] * states[s] + drive for s in range(MODES)]
        return now, one, states

    start = (
        [before(i, 1) for i in range(3)],
        [before(i, 2) for i in range(3)],
        [jnp.zeros((8, LANES), F32)] * MODES,
    )
    ends = lax.fori_loop(0, HALF, scan_one, start)[2]

    for s in range(MODES):
        e = ends[s]
        sw = swap(e)
        el = jnp.where(left, e, sw)
        er = jnp.where(left, sw, e)
        g = l64_s[s] * el + er
        for i, sh in enumerate((1, 2, 4)):
            g = g + step_s[i, s] * pltpu.roll(g, sh, 0)
        end_s[0, s] = jnp.where(sub >= 1, pltpu.roll(g, 1, 0), 0.0)
        end_s[1, s] = el
        end_s[2, s] = g
    low = jnp.concatenate([end_s[2, s, 7:8, :] for s in range(8)], axis=0)
    high = jnp.concatenate([end_s[2, s, 7:8, :] for s in range(8, 16)], axis=0)
    totals[z] = jnp.where(left, low, high)

    def st_copy(d):
        return pltpu.make_async_remote_copy(
            src_ref=totals.at[z],
            dst_ref=totals.at[z],
            send_sem=st_send.at[d],
            recv_sem=st_recv.at[d],
            device_id=(((z + d) % nz) * 8 + q, ch),
            device_id_type=MESH,
        )

    @pl.loop(1, nz)
    def _(d):
        st_copy(d).start()

    @pl.loop(1, nz)
    def _(d):
        s = (z + nz - d) % nz
        pltpu.make_async_remote_copy(
            src_ref=totals.at[s],
            dst_ref=totals.at[s],
            send_sem=st_send.at[d],
            recv_sem=st_recv.at[d],
            device_id=sib,
            device_id_type=MESH,
        ).wait_recv()

    into = jnp.zeros((8, LANES), F32)
    for s in range(nz):
        into = into + zw_s[s] * totals[s]
    into_r = swap(into)
    into_lo = jnp.where(left, into, into_r)
    into_hi = jnp.where(left, into_r, into)

    states = []
    for s in range(MODES):
        zc = (into_lo if s < 8 else into_hi)[s % 8 : s % 8 + 1, :]
        c = end_s[0, s] + pow_s[s] * zc
        states.append(jnp.where(left, c, l64_s[s] * c + end_s[1, s]))

    def scan_two(r, states):
        drive = drive_s[r]
        states = [lam_s[s] * states[s] + drive for s in range(MODES)]
        terms = [amp_s[s] * states[s] for s in range(MODES)]
        while len(terms) > 1:
            terms = [a + b for a, b in zip(terms[::2], terms[1::2])]
        obuf[pl.ds(pl.multiple_of(r * 8, 8), 8), :] = gate_s[r] * (terms[0] + skp * drive)
        return states

    lax.fori_loop(0, HALF, scan_two, states)

    for j in range(GROUP):
        outbuf[j] = obuf[pl.ds(j, HALF, stride=8), :].astype(BF16)

    def out_copy(d):
        to = (q + d) % 8
        return pltpu.make_async_remote_copy(
            src_ref=outbuf.at[to],
            dst_ref=inbox.at[q],
            send_sem=out_send.at[d],
            recv_sem=out_recv.at[d],
            device_id=(base + to, ch),
            device_id_type=MESH,
        )

    @pl.loop(1, GROUP)
    def _(d):
        out_copy(d).start()

    inbox[q] = outbuf[q]

    for copy in sent:
        copy.wait_send()
    rim_copy.wait_send()

    @pl.loop(1, nz)
    def _(d):
        st_copy(d).wait_send()

    @pl.loop(1, GROUP)
    def _(d):
        out_copy(d).wait_send()
        g = (q + 8 - d) % 8
        pltpu.make_async_remote_copy(
            src_ref=inbox.at[g],
            dst_ref=inbox.at[g],
            send_sem=out_send.at[d],
            recv_sem=out_recv.at[d],
            device_id=sib,
            device_id_type=MESH,
        ).wait_recv()

    for g in range(GROUP // 2):
        a = inbox[2 * g].astype(F32)
        b = inbox[2 * g + 1].astype(F32)
        cols = slice(g * LANES, (g + 1) * LANES)
        o_ref[0:HALF, cols] = jnp.where(left64, a, swap(b)).astype(BF16)
        o_ref[HALF:, cols] = jnp.where(left64, swap(a), b).astype(BF16)


def local(tokens, norm_gain, in_proj, short_taps, decay, residue, skip):
    rows, width = tokens.shape
    channels = in_proj.shape[2]
    nz = lax.axis_size("ctx") // GROUP
    weights = jnp.transpose(in_proj, (1, 0, 2))
    vmem = pl.BlockSpec(memory_space=pltpu.VMEM)
    dma = pltpu.SemaphoreType.DMA
    const = pltpu.VMEM((MODES, 8, LANES), F32)
    return pl.pallas_call(
        functools.partial(kernel, nz),
        out_shape=jax.ShapeDtypeStruct((rows, channels), BF16),
        in_specs=[vmem] * 7,
        out_specs=vmem,
        scratch_shapes=[
            pltpu.VMEM((GROUP, ROWS, width), BF16),
            pltpu.VMEM((GROUP, 3, 32, LANES), BF16),
            pltpu.VMEM((nz, 384, LANES), BF16),
            pltpu.VMEM((width, 2 * LANES), BF16),
            pltpu.VMEM((3, GROUP * HALF, LANES), F32),
            pltpu.VMEM((3, 8, LANES), F32),
            pltpu.VMEM((HALF, 8, LANES), F32),
            pltpu.VMEM((HALF, 8, LANES), F32),
            const,
            const,
            const,
            pltpu.VMEM((3, MODES, 8, LANES), F32),
            const,
            pltpu.VMEM((nz, 8, LANES), F32),
            pltpu.VMEM((3, MODES, 8, LANES), F32),
            pltpu.VMEM((nz, 8, LANES), F32),
            pltpu.VMEM((GROUP * HALF, LANES), F32),
            pltpu.VMEM((GROUP, HALF, LANES), BF16),
            pltpu.VMEM((GROUP, HALF, LANES), BF16),
            dma((8,)),
            dma((8,)),
            dma((64,)),
            dma((32,)),
            dma((32,)),
            dma((8,)),
            dma((8,)),
            dma((8,)),
            dma((8,)),
            dma((2,)),
            dma((16,)),
            dma((16,)),
            dma((8,)),
            dma((8,)),
        ],
        compiler_params=pltpu.CompilerParams(
            collective_id=0, has_side_effects=True, vmem_limit_bytes=48 * 1024 * 1024
        ),
        name="hyena",
    )(
        tokens,
        norm_gain.reshape(1, width),
        weights,
        short_taps.reshape(9, channels),
        decay,
        residue,
        skip.reshape(1, channels),
    )


def solution(mesh):
    placed = (
        P("ctx", None),
        P(),
        P("ctx", None, "ch"),
        P(None, None, "ch"),
        P(None, "ch"),
        P(None, "ch"),
        P("ch"),
    )
    return jax.shard_map(
        local, mesh=mesh, in_specs=placed, out_specs=P("ctx", "ch"), check_vma=False
    )
```

time: 814 us -> 87.2 us (0.11)
  waiting for transfers between devices: 639 us -> 0 us
  Pallas kernels: 0 us -> 82.5 us
  blocking collectives: 62.8 us -> 0 us
  other arithmetic: 26.5 us -> 0 us
  starting transfers between devices: 26 us -> 0 us
  local copies, waits for them, and re-layouts: 23.4 us -> 4.33 us
  matrix products: 18.1 us -> 0 us
  between operations: 13.7 us -> 0.05 us
    all_gather x1 -> x0, waiting for transfers between devices: 612 us -> none  [local(): weight_piece = lax.all_gather(in_proj, 'ctx', axis=0, tiled=True)]
    pallas_call x0 -> x1, Pallas kernels: none -> 82.5 us  [local(): pl.pallas_call(functools.partial(kernel, nz), out_shape=jax.ShapeDtypeStr...]
    all_to_all x2 -> x0, blocking collectives: 62.8 us -> none  [the longest x1 40.1 us: local(): lax.all_to_all(shortened(jnp.stack([back_real, back_imag])), 'ctx', split...]
    all_to_all x2 -> x0, starting transfers between devices: 22.6 us -> none  [the longest x1 16.9 us: local(): lax.all_to_all(regrouped.astype(jnp.bfloat16), 'ctx', split_axis=0, conca...]
    dot_general x13 -> x0, matrix products: 18.1 us -> none  [the longest x1 8.89 us: local(): projected = jnp.dot(normed, flat_piece, preferred_element_type=jnp.float32)]
    all_gather x1 -> x0, local copies, waits for them, and re-layouts: 17 us -> none  [local(): weight_piece = lax.all_gather(in_proj, 'ctx', axis=0, tiled=True)]
    all_to_all x2 -> x0, waiting for transfers between devices: 17 us -> none  [the longest x1 16.6 us: local(): lax.all_to_all(regrouped.astype(jnp.bfloat16), 'ctx', split_axis=0, conca...]
    mul x65 -> x0, other arithmetic: 15.6 us -> none  [the longest x16 12.2 us: add_mode(): amplitude = residue_cols[mode] * jnp.sqrt(2.0 * rate)]
  transfers between devices with their start and end apart: 4 -> 0, of which waited for: 4 -> 0; matrix products, arithmetic and copies ran while one was open for 3% -> 0% of each run, Pallas kernels for 0% -> 0%
where the time goes in v1:
time: 87.2 us; the launch traced here: 86.9 us
  Pallas kernels  82.5 us (95%)
  local copies, waits for them, and re-layouts  4.33 us (5%)
    pallas_call x1, Pallas kernels, local(): pl.pallas_call(functools.partial(kernel, nz), out_shape=jax.ShapeDtypeStr...  82.5 us
    unnamed x13, local copies, waits for them, and re-layouts  3.54 us

profile of v1, /device:TPU:8, one launch (start us, length us, event | category | flops | bytes accessed | tf_op | source)
XLA Modules:
  0.0 86.9 jit_solution(15805057097968868279)
XLA Ops:
  0.0 0.0 copy-start.2
  0.0 0.0 copy-start.4
  0.0 0.0 copy-start.5
  0.0 0.8 reshape.10.taps_ref
  0.8 0.0 copy-done.2
  0.8 0.0 copy-done.4
  0.8 0.0 copy-done.5
  0.8 0.0 copy-start
  0.8 1.2 %copy-done = bf16[128,4096]{1,0:T(8,128)(2,1)S(1)} copy-done((bf16[128,4096]{1,0:T(8,128)(2,1)S(1)}, bf16[128,4096]{1,0:T(8,128)(2,1)}, u32[]{:S(2)}) %copy-start) | copy-done | bytes 1048600
  2.1 0.0 copy-start.1
  2.1 0.9 %copy-done.1 = bf16[32,3,512]{2,0,1:T(8,128)(2,1)S(1)} copy-done((bf16[32,3,512]{2,0,1:T(8,128)(2,1)S(1)}, bf16[32,3,512]{2,0,1:T(8,128)(2,1)}, u32[]{:S(2)}) %copy-start.1) | copy-done | bytes 98328
  2.9 0.0 copy-start.3
  3.0 0.8 copy-done.3
  3.7 82.5 %hyena.1 = bf16[128,512]{1,0:T(8,128)(2,1)S(1)} custom-call(bf16[128,4096]{1,0:T(8,128)(2,1)S(1)} %copy-done, f32[1,4096]{1,0:T(1,128)S(1)} %bitcast.4, bf16[3,32,512]{2,1,0:T(8,128)(2,1)S(1)} %bitcast.3, f32[9,512]{1,0:T(8,128)S(1)} %reshape.10.taps_ref, f32[16,512]{1,0:T(8,128)S(1)} %copy-done.2, f32[16,512]{1,0:T(8,128)S(1)} %copy-done.3, ...), custom_call_target="tpu_custom_call" | custom-call | tf_op jit(solution)/shard_map/hyena/pallas_call | solution.py:544
  86.2 0.7 copy.9
Async XLA Ops:
  0.0 0.8 copy-start.2
  0.0 0.8 copy-start.4
  0.0 0.8 copy-start.5
  0.8 1.2 %copy-start = (bf16[128,4096]{1,0:T(8,128)(2,1)S(1)}, bf16[128,4096]{1,0:T(8,128)(2,1)}, u32[]{:S(2)}) copy-start(bf16[128,4096]{1,0:T(8,128)(2,1)} %tok_ref.1) | copy-start | bytes 3145732
  2.1 0.9 %copy-start.1 = (bf16[32,3,512]{2,0,1:T(8,128)(2,1)S(1)}, bf16[32,3,512]{2,0,1:T(8,128)(2,1)}, u32[]{:S(2)}) copy-start(bf16[32,3,512]{2,0,1:T(8,128)(2,1)} %param.9) | copy-start | bytes 294916
  2.9 0.8 copy-start.3

commit v2 on v1

--- a/solution.py
+++ b/solution.py
@@ -21,24 +21,32 @@
 
 def kernel(
     nz,
+    tok_hbm,
+    gain_hbm,
+    w_hbm,
+    taps_hbm,
+    dec_hbm,
+    res_hbm,
+    skip_hbm,
+    o_ref,
     tok_ref,
     gain_ref,
-    w_ref,
     taps_ref,
     dec_ref,
     res_ref,
     skip_ref,
-    o_ref,
     X,
     wa,
     slabs,
     wfull,
+    part,
     proj,
     rim,
     drive_s,
     gate_s,
     lam_s,
     amp_s,
+    l62_s,
     l64_s,
     step_s,
     pow_s,
@@ -48,6 +56,7 @@
     obuf,
     outbuf,
     inbox,
+    in_sem,
     wa_send,
     wa_recv,
     tok_send,
@@ -90,6 +99,27 @@
     z_dn = (((z + nz - 1) % nz) * 8 + q, ch)
     y_far = (base + plane(1 - y_lo, x), (1 - y_hi) * 2 + core)
 
+    def half_rows(half):
+        return pl.ds(pl.multiple_of(half * HALF, HALF), HALF)
+
+    fetch = [
+        pltpu.make_async_copy(tok_hbm.at[half_rows(core), :], tok_ref.at[half_rows(core), :], in_sem.at[0]),
+        pltpu.make_async_copy(gain_hbm, gain_ref, in_sem.at[1]),
+        pltpu.make_async_copy(
+            w_hbm.at[:, :, pl.ds(pl.multiple_of(tile * LANES, LANES), LANES)], wa.at[q], in_sem.at[2]
+        ),
+        pltpu.make_async_copy(
+            tok_hbm.at[half_rows(1 - core), :], tok_ref.at[half_rows(1 - core), :], in_sem.at[3]
+        ),
+        pltpu.make_async_copy(dec_hbm, dec_ref, in_sem.at[4]),
+        pltpu.make_async_copy(res_hbm, res_ref, in_sem.at[5]),
+        pltpu.make_async_copy(taps_hbm, taps_ref, in_sem.at[6]),
+        pltpu.make_async_copy(skip_hbm, skip_ref, in_sem.at[7]),
+    ]
+    for copy in fetch:
+        copy.start()
+    totals[...] = jnp.zeros_like(totals)
+
     barrier = pltpu.get_barrier_semaphore()
 
     def greet(dev):
@@ -134,6 +164,8 @@
         ms = jnp.mean(v * v, axis=1, keepdims=True)
         X[j_own, rows, :] = (v * lax.rsqrt(ms + 1e-06) * gain_ref[...]).astype(BF16)
 
+    fetch[0].wait()
+    fetch[1].wait()
     norm(core, 0)
     norm(core, 2)
     pl.semaphore_wait(barrier, 7 + (nz - 1) + 2)
@@ -144,7 +176,7 @@
         to = (q + d) % 8
         lanes = pl.ds(pl.multiple_of((to // 2) * LANES, LANES), LANES)
         return pltpu.make_async_remote_copy(
-            src_ref=w_ref.at[:, :, lanes],
+            src_ref=w_hbm.at[:, :, lanes],
             dst_ref=wa.at[q],
             send_sem=wa_send.at[d],
             recv_sem=wa_recv.at[d],
@@ -213,52 +245,57 @@
     send(j_own, 3, x_up)
     send(j_own, 1, x_dn)
 
-    wa[q] = w_ref[:, :, pl.ds(pl.multiple_of(tile * LANES, LANES), LANES)]
+    fetch[2].wait()
 
     @pl.loop(1, GROUP)
     def _(d):
-        copy = wa_copy(d)
+        ref = wa.at[(q + 8 - d) % 8]
         pltpu.make_async_remote_copy(
-            src_ref=wa.at[(q + 8 - d) % 8],
-            dst_ref=wa.at[(q + 8 - d) % 8],
+            src_ref=ref,
+            dst_ref=ref,
             send_sem=wa_send.at[d],
             recv_sem=wa_recv.at[d],
             device_id=sib,
             device_id_type=MESH,
         ).wait_recv()
-        copy.wait_send()
 
     lane32 = lax.broadcasted_iota(jnp.int32, (32, LANES), 1)
     left32 = lane32 < HALF
-    for g in range(GROUP):
-        qk = jnp.where(left32, pick(wa[g, 0].astype(F32), left32), pick(wa[g, 1].astype(F32), left32))
-        slabs[z, g * 32 : (g + 1) * 32, :] = qk.astype(BF16)
-    for g in range(GROUP // 2):
-        v = jnp.where(
-            left32, pick(wa[g, 2].astype(F32), left32), pick(wa[g + 4, 2].astype(F32), left32)
-        )
-        slabs[z, 256 + g * 32 : 256 + (g + 1) * 32, :] = v.astype(BF16)
-
-    def z_copy(step, up):
+
+    CHUNK = 128
+
+    def z_ref(s, k):
+        return slabs.at[s, pl.ds(k * CHUNK, CHUNK), :]
+
+    def z_copy(step, up, k):
         s = (z + nz - step) % nz if up else (z + step) % nz
         sems, recvs = (zp_send, zp_recv) if up else (zm_send, zm_recv)
         return pltpu.make_async_remote_copy(
-            src_ref=slabs.at[s],
-            dst_ref=slabs.at[s],
-            send_sem=sems.at[step],
-            recv_sem=recvs.at[step],
+            src_ref=z_ref(s, k),
+            dst_ref=z_ref(s, k),
+            send_sem=sems.at[step * 3 + k],
+            recv_sem=recvs.at[step * 3 + k],
             device_id=z_up if up else z_dn,
             device_id_type=MESH,
         )
 
-    def z_arrived(step, up):
+    n_up = nz // 2
+    n_dn = nz - 1 - n_up
+
+    def z_send(step, up, k):
+        if step < (n_up if up else n_dn):
+            copy = z_copy(step, up, k)
+            copy.start()
+            sent.append(copy)
+
+    def z_arrived(step, up, k):
         s = (z + 2 * nz - step - 1) % nz if up else (z + step + 1) % nz
         sems, recvs = (zp_send, zp_recv) if up else (zm_send, zm_recv)
         pltpu.make_async_remote_copy(
-            src_ref=slabs.at[s],
-            dst_ref=slabs.at[s],
-            send_sem=sems.at[step],
-            recv_sem=recvs.at[step],
+            src_ref=z_ref(s, k),
+            dst_ref=z_ref(s, k),
+            send_sem=sems.at[step * 3 + k],
+            recv_sem=recvs.at[step * 3 + k],
             device_id=z_up if up else z_dn,
             device_id_type=MESH,
         ).wait_recv()
@@ -271,74 +308,77 @@
         wfull[pl.ds(at, 128), LANES:] = v
         wfull[pl.ds(at + 128, 128), LANES:] = swap(v.astype(F32)).astype(BF16)
 
-    n_up = nz // 2
-    n_dn = nz - 1 - n_up
-
-    def z_start(step):
-        for up, most in ((True, n_up), (False, n_dn)):
-            if step < most:
-                copy = z_copy(step, up)
-                copy.start()
-                sent.append(copy)
+    for k in range(3):
+        for g in range(4):
+            if k < 2:
+                n = k * 4 + g
+                rows = jnp.where(left32, pick(wa[n, 0].astype(F32), left32), pick(wa[n, 1].astype(F32), left32))
+            else:
+                rows = jnp.where(
+                    left32, pick(wa[g, 2].astype(F32), left32), pick(wa[g + 4, 2].astype(F32), left32)
+                )
+            slabs[z, k * CHUNK + g * 32 : k * CHUNK + (g + 1) * 32, :] = rows.astype(BF16)
+        z_send(0, True, k)
+        z_send(0, False, k)
 
     def z_round(step):
         got = []
-        for up, most in ((True, n_up), (False, n_dn)):
-            if step < most:
-                got.append(z_arrived(step, up))
-        z_start(step + 1)
+        for k in range(3):
+            for up, most in ((True, n_up), (False, n_dn)):
+                if step < most:
+                    s = z_arrived(step, up, k)
+                    z_send(step + 1, up, k)
+                    if k == 0:
+                        got.append(s)
         return got
 
-    z_start(0)
-
-    for piece in range(4):
-        norm(1 - core, piece)
-    unpack(z)
-
+    for copy in fetch[3:]:
+        copy.wait()
     lanes_q = pl.ds(pl.multiple_of(tile * LANES, LANES), LANES)
     lane16 = lax.broadcasted_iota(jnp.int32, (MODES, LANES), 1)
     left16 = lane16 < HALF
-    dec = pick(dec_ref[:, lanes_q], left16)
-    res = pick(res_ref[:, lanes_q], left16)
-    skp = pick(skip_ref[:, lanes_q] * jnp.ones((8, LANES), F32), left)
-    amp = res * jnp.sqrt(2.0 * dec)
-    lam = jnp.exp(-dec)
-    l64 = jnp.exp(-dec * 64.0)
     ones8 = jnp.ones((8, LANES), F32)
     subf = sub.astype(F32)
 
-    def constants():
-        for s in range(MODES):
+    def constants(first):
+        dec = pick(dec_ref[:, lanes_q], left16)
+        amp = pick(res_ref[:, lanes_q], left16) * jnp.sqrt(2.0 * dec)
+        for s in range(first, first + 4):
             d8 = dec[s : s + 1, :] * ones8
-            lam_s[s] = lam[s : s + 1, :] * ones8
             amp_s[s] = amp[s : s + 1, :] * ones8
-            l64_s[s] = l64[s : s + 1, :] * ones8
+            lam_s[s] = jnp.exp(-d8)
+            l62_s[s] = jnp.exp(-d8 * 62.0)
+            l64_s[s] = jnp.exp(-d8 * 64.0)
             for i, sh in enumerate((1, 2, 4)):
                 step_s[i, s] = jnp.where(sub >= sh, jnp.exp(-d8 * (128.0 * sh)), 0.0)
             pow_s[s] = jnp.exp(-d8 * (128.0 * subf))
+
+    def z_weights():
+        dec = pick(dec_ref[:, lanes_q], left16)
         dec_p = jnp.where(left, dec[0:8, :], dec[8:16, :])
         for s in range(nz):
             gap = (z - 1 - s).astype(F32)
             zw_s[s] = jnp.where(s < z, jnp.exp(-dec_p * (1024.0 * jnp.maximum(gap, 0.0))), 0.0)
 
-    rounds = [
-        [(j_dn, 0, (x_up, y_up)), (j_up, 2, (x_dn, y_dn)), (p_own, 0, ()), (p_own, 2, ())],
-        [(j_dn, 1, (x_up, y_up)), (j_up, 3, (x_dn, y_dn)), (p_own, 1, ()), (p_own, 3, ())],
-        [(j_dn, 2, (y_dn,)), (j_up, 0, (y_up,)), (p_dn, 0, ()), (p_up, 2, ())],
-        [(j_dn, 3, (y_dn,)), (j_up, 1, (y_up,)), (p_dn, 1, ()), (p_up, 3, ())],
-        [(j_op, 0, (y_up,)), (j_op, 2, (y_dn,)), (p_up, 0, ()), (p_dn, 2, ())],
-        [(j_op, 1, (y_up,)), (j_op, 3, (y_dn,)), (p_up, 1, ()), (p_dn, 3, ())],
-        [(p_op, 0, ()), (p_op, 2, ())],
-        [(p_op, 1, ()), (p_op, 3, ())],
-    ]
-
     left64 = lax.broadcasted_iota(jnp.int32, (HALF, LANES), 1) < HALF
 
-    def project(j):
-        acc = jnp.dot(X[j], wfull[...], preferred_element_type=F32)
+    def products(j, lo, hi):
+        acc = None
+        for d in range(lo, hi + 1):
+            at = pl.multiple_of(((z + nz + d) % nz) * 256, 256)
+            term = jnp.dot(X[j, :, pl.ds(at, 256)], wfull[pl.ds(at, 256), :], preferred_element_type=F32)
+            acc = term if acc is None else acc + term
+        return acc
+
+    def here(j):
+        if j is not j_own:
+            for piece in range(4):
+                arrive_sib(j, piece)
+
+    def finish(j, acc):
         t0a, t0b = acc[0:HALF, 0:LANES], acc[HALF:, 0:LANES]
         t1a, t1b = acc[0:HALF, LANES:], acc[HALF:, LANES:]
-        rows = pl.ds(pl.multiple_of(j * HALF, HALF), HALF)
+        rows = half_rows(j)
         for i, v in enumerate(
             (
                 jnp.where(left64, t0a, swap(t0b)),
@@ -348,33 +388,74 @@
         ):
             proj[i, rows, :] = v.astype(BF16).astype(F32)
 
-    def project_when_here(j):
-        for piece in range(4):
-            arrive_sib(j, piece)
-        project(j)
-
-    for r, events in enumerate(rounds):
-        got = z_round(r) if r < 7 else []
-        for j, piece, onward in events:
+    units = [
+        [(j_dn, 0, (x_up, y_up)), (j_up, 2, (x_dn, y_dn)), (p_own, 0, ()), (p_own, 2, ())],
+        [(j_dn, 1, (x_up, y_up)), (j_up, 3, (x_dn, y_dn)), (p_own, 1, ()), (p_own, 3, ())],
+        [(j_dn, 2, (y_dn,)), (j_up, 0, (y_up,)), (p_dn, 0, ()), (p_up, 2, ())],
+        [(j_dn, 3, (y_dn,)), (j_up, 1, (y_up,)), (p_dn, 1, (x_up,)), (p_up, 3, (x_dn,))],
+        [(j_op, 0, (y_up,)), (j_op, 2, (y_dn,)), (p_up, 0, ()), (p_dn, 2, ())],
+        [(j_op, 1, ()), (j_op, 3, ()), (p_up, 1, ()), (p_dn, 3, ())],
+        [(p_op, 0, ()), (p_op, 2, ()), (p_op, 1, ()), (p_op, 3, ())],
+    ]
+    waiting = []
+
+    def unit(u):
+        for j, piece, onward in units[u]:
             arrive(j, piece)
             for dev in onward:
                 send(j, piece, dev)
+            waiting.append((j, piece))
+
+    def to_sibling():
+        for j, piece in waiting:
             send(j, piece, sib)
+        waiting.clear()
+
+    norm(1 - core, 0)
+    norm(1 - core, 1)
+    unpack(z)
+    unit(0)
+    for r in range(8):
+        got = z_round(r)
+        to_sibling()
         for s in got:
             unpack(s)
         if r == 0:
-            constants()
-        if r == 6:
-            for s in z_round(7):
-                unpack(s)
-            project(j_own)
-            project_when_here(p_own)
-            project_when_here(j_dn)
-            project_when_here(j_up)
-    project_when_here(j_op)
-    project_when_here(p_up)
-    project_when_here(p_dn)
-    project_when_here(p_op)
+            norm(1 - core, 2)
+            norm(1 - core, 3)
+            unit(1)
+        elif r == 1:
+            constants(0)
+            unit(2)
+        elif r == 2:
+            constants(4)
+            constants(8)
+        elif r == 3:
+            constants(12)
+            unit(3)
+        elif r == 4:
+            z_weights()
+            unit(4)
+        elif r == 5:
+            for j in (j_own, p_own):
+                here(j)
+                part[j] = products(j, -6, 6)
+            unit(5)
+        elif r == 6:
+            for j in (j_dn, j_up):
+                here(j)
+                part[j] = products(j, -7, 7)
+            unit(6)
+            to_sibling()
+            for j in (j_op, p_up, p_dn):
+                here(j)
+                part[j] = products(j, -7, 7)
+    for j in (j_own, p_own):
+        finish(j, part[j] + products(j, -8, -7) + products(j, 7, 7))
+    for j in (j_dn, j_up, j_op, p_up, p_dn):
+        finish(j, part[j] + products(j, -8, -8))
+    here(p_op)
+    finish(p_op, products(p_op, -8, 7))
 
     rim_copy = pltpu.make_async_remote_copy(
         src_ref=proj.at[:, 504:512, :],
@@ -385,27 +466,25 @@
         device_id_type=MESH,
     )
     rim_copy.start()
-    rim_copy.wait_recv()
 
     def at_step(i, r):
         return proj[i, pl.ds(r, 8, stride=HALF), :]
 
-    def before(i, back):
+    def before(i, back, edge):
         last = swap(at_step(i, HALF - back))
-        edge = swap(rim[i, 8 - back : 9 - back, :] * ones8)
-        edge = jnp.where(z == 0, 0.0, edge)
         shifted = jnp.where(sub == 0, edge, pltpu.roll(last, 1, 0))
         return jnp.where(left, shifted, last)
 
-    taps = [
-        [pick(taps_ref[3 * k + i : 3 * k + i + 1, lanes_q] * ones8, left) for i in range(3)]
-        for k in range(3)
-    ]
+    taps = [[pick(taps_ref[k, i : i + 1, lanes_q] * ones8, left) for i in range(3)] for k in range(3)]
+    skp = pick(skip_ref[:, lanes_q] * ones8, left)
+
+    def featurize(now, one, two):
+        return [taps[0][i] * now[i] + taps[1][i] * one[i] + taps[2][i] * two[i] for i in range(3)]
 
     def scan_one(r, carry):
         one, two, states = carry
         now = [at_step(i, r) for i in range(3)]
-        feats = [taps[0][i] * now[i] + taps[1][i] * one[i] + taps[2][i] * two[i] for i in range(3)]
+        feats = featurize(now, one, two)
         drive = feats[1] * feats[2]
         drive_s[r] = drive
         gate_s[r] = feats[0]
@@ -413,14 +492,31 @@
         return now, one, states
 
     start = (
-        [before(i, 1) for i in range(3)],
-        [before(i, 2) for i in range(3)],
+        [before(i, 1, 0.0) for i in range(3)],
+        [before(i, 2, 0.0) for i in range(3)],
         [jnp.zeros((8, LANES), F32)] * MODES,
     )
-    ends = lax.fori_loop(0, HALF, scan_one, start)[2]
+    ends = lax.fori_loop(0, HALF, scan_one, start, unroll=2)[2]
+
+    rim_copy.wait_recv()
+
+    def edge(i, back):
+        return jnp.where(z == 0, 0.0, swap(rim[i, 8 - back : 9 - back, :] * ones8))
+
+    one = [before(i, 1, edge(i, 1)) for i in range(3)]
+    two = [before(i, 2, edge(i, 2)) for i in range(3)]
+    now = [at_step(i, 0) for i in range(3)]
+    changes = []
+    for r in range(2):
+        feats = featurize(now, one, two)
+        drive = feats[1] * feats[2]
+        changes.append(drive - drive_s[r])
+        drive_s[r] = drive
+        gate_s[r] = feats[0]
+        two, one, now = one, now, [at_step(i, 1) for i in range(3)]
 
     for s in range(MODES):
-        e = ends[s]
+        e = ends[s] + l62_s[s] * (lam_s[s] * changes[0] + changes[1])
         sw = swap(e)
         el = jnp.where(left, e, sw)
         er = jnp.where(left, sw, e)
@@ -444,21 +540,34 @@
             device_id_type=MESH,
         )
 
-    @pl.loop(1, nz)
+    far_first = sorted(range(1, nz), key=lambda d: -min(d, nz - d))
+    for d in far_first:
+
+        @pl.when(z + d < nz)
+        def _(d=d):
+            st_copy(d).start()
+
+    for copy in sent:
+        copy.wait_send()
+    rim_copy.wait_send()
+
+    @pl.loop(1, GROUP)
     def _(d):
-        st_copy(d).start()
-
-    @pl.loop(1, nz)
-    def _(d):
-        s = (z + nz - d) % nz
-        pltpu.make_async_remote_copy(
-            src_ref=totals.at[s],
-            dst_ref=totals.at[s],
-            send_sem=st_send.at[d],
-            recv_sem=st_recv.at[d],
-            device_id=sib,
-            device_id_type=MESH,
-        ).wait_recv()
+        wa_copy(d).wait_send()
+
+    for d in range(1, nz):
+
+        @pl.when(z >= d)
+        def _(d=d):
+            s = (z + nz - d) % nz
+            pltpu.make_async_remote_copy(
+                src_ref=totals.at[s],
+                dst_ref=totals.at[s],
+                send_sem=st_send.at[d],
+                recv_sem=st_recv.at[d],
+                device_id=sib,
+                device_id_type=MESH,
+            ).wait_recv()
 
     into = jnp.zeros((8, LANES), F32)
     for s in range(nz):
@@ -482,7 +591,7 @@
         obuf[pl.ds(pl.multiple_of(r * 8, 8), 8), :] = gate_s[r] * (terms[0] + skp * drive)
         return states
 
-    lax.fori_loop(0, HALF, scan_two, states)
+    lax.fori_loop(0, HALF, scan_two, states, unroll=2)
 
     for j in range(GROUP):
         outbuf[j] = obuf[pl.ds(j, HALF, stride=8), :].astype(BF16)
@@ -498,32 +607,29 @@
             device_id_type=MESH,
         )
 
+    for d in (6, 2, 7, 5, 3, 1, 4):
+        out_copy(d).start()
+
+    inbox[q] = outbuf[q]
+
+    for d in range(1, nz):
+
+        @pl.when(z + d < nz)
+        def _(d=d):
+            st_copy(d).wait_send()
+
     @pl.loop(1, GROUP)
     def _(d):
-        out_copy(d).start()
-
-    inbox[q] = outbuf[q]
-
-    for copy in sent:
-        copy.wait_send()
-    rim_copy.wait_send()
-
-    @pl.loop(1, nz)
-    def _(d):
-        st_copy(d).wait_send()
-
-    @pl.loop(1, GROUP)
-    def _(d):
-        out_copy(d).wait_send()
-        g = (q + 8 - d) % 8
+        ref = inbox.at[(q + 8 - d) % 8]
         pltpu.make_async_remote_copy(
-            src_ref=inbox.at[g],
-            dst_ref=inbox.at[g],
+            src_ref=ref,
+            dst_ref=ref,
             send_sem=out_send.at[d],
             recv_sem=out_recv.at[d],
             device_id=sib,
             device_id_type=MESH,
         ).wait_recv()
+        out_copy(d).wait_send()
 
     for g in range(GROUP // 2):
         a = inbox[2 * g].astype(F32)
@@ -544,17 +650,25 @@
     return pl.pallas_call(
         functools.partial(kernel, nz),
         out_shape=jax.ShapeDtypeStruct((rows, channels), BF16),
-        in_specs=[vmem] * 7,
+        in_specs=[pl.BlockSpec(memory_space=pl.ANY)] * 7,
         out_specs=vmem,
         scratch_shapes=[
+            pltpu.VMEM((rows, width), BF16),
+            pltpu.VMEM((1, width), F32),
+            pltpu.VMEM((3, 3, channels), F32),
+            pltpu.VMEM((MODES, channels), F32),
+            pltpu.VMEM((MODES, channels), F32),
+            pltpu.VMEM((1, channels), F32),
             pltpu.VMEM((GROUP, ROWS, width), BF16),
             pltpu.VMEM((GROUP, 3, 32, LANES), BF16),
             pltpu.VMEM((nz, 384, LANES), BF16),
             pltpu.VMEM((width, 2 * LANES), BF16),
+            pltpu.VMEM((GROUP, ROWS, 2 * LANES), F32),
             pltpu.VMEM((3, GROUP * HALF, LANES), F32),
             pltpu.VMEM((3, 8, LANES), F32),
             pltpu.VMEM((HALF, 8, LANES), F32),
             pltpu.VMEM((HALF, 8, LANES), F32),
+            const,
             const,
             const,
             const,
@@ -568,13 +682,14 @@
             pltpu.VMEM((GROUP, HALF, LANES), BF16),
             dma((8,)),
             dma((8,)),
+            dma((8,)),
             dma((64,)),
             dma((32,)),
             dma((32,)),
-            dma((8,)),
-            dma((8,)),
-            dma((8,)),
-            dma((8,)),
+            dma((24,)),
+            dma((24,)),
+            dma((24,)),
+            dma((24,)),
             dma((2,)),
             dma((16,)),
             dma((16,)),
@@ -582,14 +697,14 @@
             dma((8,)),
         ],
         compiler_params=pltpu.CompilerParams(
-            collective_id=0, has_side_effects=True, vmem_limit_bytes=48 * 1024 * 1024
+            collective_id=0, has_side_effects=True, vmem_limit_bytes=56 * 1024 * 1024
         ),
         name="hyena",
     )(
         tokens,
         norm_gain.reshape(1, width),
         weights,
-        short_taps.reshape(9, channels),
+        short_taps,
         decay,
         residue,
         skip.reshape(1, channels),

time: 87.2 us -> 67.1 us (0.77)
  the two profiles are of different devices: /device:TPU:8 before, /device:TPU:32 now
where the time goes in v2:
time: 67.1 us; the launch traced here: 67 us
  Pallas kernels  65.4 us (97%)
  local copies, waits for them, and re-layouts  1.57 us (2%)
    pallas_call x1, Pallas kernels, local(): pl.pallas_call(functools.partial(kernel, nz), out_shape=jax.ShapeDtypeStr...  65.4 us
    unnamed x1, local copies, waits for them, and re-layouts  1.57 us

profile of v2, /device:TPU:32, one launch (start us, length us, event | category | flops | bytes accessed | tf_op | source)
XLA Modules:
  0.0 67.0 jit_solution(2240493930638382466)
XLA Ops:
  0.0 65.4 %hyena.1 = bf16[128,512]{1,0:T(8,128)(2,1)} custom-call(bf16[128,4096]{1,0:T(8,128)(2,1)} %tok_hbm.1, f32[1,4096]{1,0:T(1,128)} %bitcast.4, bf16[3,32,512]{2,1,0:T(8,128)(2,1)} %bitcast.3, f32[3,3,512]{2,1,0:T(4,128)} %taps_hbm.1, f32[16,512]{1,0:T(8,128)} %dec_hbm.1, f32[16,512]{1,0:T(8,128)} %res_hbm.1, f32[1,512]{1,0:T(1,128)} %bitcast.5), custom_call_target="tpu_custom_call" | custom-call | tf_op jit(solution)/shard_map/hyena/pallas_call | solution.py:650
  65.4 1.6 %copy.9 = bf16[128,512]{1,0:T(8,128)(2,1)} copy(bf16[128,512]{1,0:T(8,128)(2,1)} %hyena.1) | data formatting | bytes 262144

commit v3 on v2

--- a/solution.py
+++ b/solution.py
@@ -31,6 +31,7 @@
     o_ref,
     tok_ref,
     gain_ref,
+    w_ref,
     taps_ref,
     dec_ref,
     res_ref,
@@ -66,6 +67,8 @@
     zp_recv,
     zm_send,
     zm_recv,
+    sl_send,
+    sl_recv,
     rim_sem,
     st_send,
     st_recv,
@@ -102,22 +105,23 @@
     def half_rows(half):
         return pl.ds(pl.multiple_of(half * HALF, HALF), HALF)
 
-    fetch = [
-        pltpu.make_async_copy(tok_hbm.at[half_rows(core), :], tok_ref.at[half_rows(core), :], in_sem.at[0]),
-        pltpu.make_async_copy(gain_hbm, gain_ref, in_sem.at[1]),
-        pltpu.make_async_copy(
-            w_hbm.at[:, :, pl.ds(pl.multiple_of(tile * LANES, LANES), LANES)], wa.at[q], in_sem.at[2]
-        ),
-        pltpu.make_async_copy(
-            tok_hbm.at[half_rows(1 - core), :], tok_ref.at[half_rows(1 - core), :], in_sem.at[3]
-        ),
-        pltpu.make_async_copy(dec_hbm, dec_ref, in_sem.at[4]),
-        pltpu.make_async_copy(res_hbm, res_ref, in_sem.at[5]),
-        pltpu.make_async_copy(taps_hbm, taps_ref, in_sem.at[6]),
-        pltpu.make_async_copy(skip_hbm, skip_ref, in_sem.at[7]),
-    ]
+    pairs = (
+        (tok_hbm.at[half_rows(core), :], tok_ref.at[half_rows(core), :]),
+        (gain_hbm, gain_ref),
+        (w_hbm, w_ref),
+        (tok_hbm.at[half_rows(1 - core), :], tok_ref.at[half_rows(1 - core), :]),
+        (dec_hbm, dec_ref),
+        (res_hbm, res_ref),
+        (taps_hbm, taps_ref),
+        (skip_hbm, skip_ref),
+    )
+    fetch = [pltpu.make_async_copy(a, b, in_sem.at[i]) for i, (a, b) in enumerate(pairs)]
     for copy in fetch:
         copy.start()
+
+    def w_lanes(chip):
+        return pl.ds(pl.multiple_of((chip // 2) * LANES, LANES), LANES)
+
     totals[...] = jnp.zeros_like(totals)
 
     barrier = pltpu.get_barrier_semaphore()
@@ -128,6 +132,7 @@
     @pl.loop(1, GROUP)
     def _(d):
         greet((base + (q + d) % 8, ch))
+        greet((base + (q + d) % 8, y_hi * 2 + (1 - core)))
 
     @pl.loop(1, nz)
     def _(d):
@@ -168,25 +173,29 @@
     fetch[1].wait()
     norm(core, 0)
     norm(core, 2)
-    pl.semaphore_wait(barrier, 7 + (nz - 1) + 2)
+    fetch[2].wait()
+    pl.semaphore_wait(barrier, 7 + 7 + (nz - 1) + 2)
 
     sent = []
 
     def wa_copy(d):
         to = (q + d) % 8
-        lanes = pl.ds(pl.multiple_of((to // 2) * LANES, LANES), LANES)
         return pltpu.make_async_remote_copy(
-            src_ref=w_hbm.at[:, :, lanes],
-            dst_ref=wa.at[q],
+            src_ref=w_ref.at[:, :, w_lanes(to)],
+            dst_ref=wa.at[core, q],
             send_sem=wa_send.at[d],
-            recv_sem=wa_recv.at[d],
-            device_id=(base + to, ch),
+            recv_sem=wa_recv.at[core * 8 + d],
+            device_id=(base + to, y_hi * 2 + 1),
             device_id_type=MESH,
         )
 
     @pl.loop(1, GROUP)
     def _(d):
         wa_copy(d).start()
+
+    @pl.when(core == 0)
+    def _():
+        wa_copy(0).start()
 
     count = [0]
 
@@ -205,8 +214,8 @@
             device_id_type=MESH,
         )
         count[0] += 1
-        copy.start()
         sent.append(copy)
+        return copy
 
     def arrive(j, piece):
         ref = piece_ref(j, core, piece)
@@ -230,107 +239,132 @@
             device_id_type=MESH,
         ).wait_recv()
 
-    send(j_own, 0, x_up)
-    send(j_own, 2, x_dn)
-    send(j_own, 0, y_up)
-    send(j_own, 2, y_dn)
+    send(j_own, 0, x_up).start()
+    send(j_own, 2, x_dn).start()
+    send(j_own, 0, y_up).start()
+    send(j_own, 2, y_dn).start()
     norm(core, 1)
     norm(core, 3)
-    send(j_own, 1, x_up)
-    send(j_own, 3, x_dn)
-    send(j_own, 1, y_up)
-    send(j_own, 3, y_dn)
-    send(j_own, 2, x_up)
-    send(j_own, 0, x_dn)
-    send(j_own, 3, x_up)
-    send(j_own, 1, x_dn)
-
-    fetch[2].wait()
-
-    @pl.loop(1, GROUP)
-    def _(d):
-        ref = wa.at[(q + 8 - d) % 8]
-        pltpu.make_async_remote_copy(
+    send(j_own, 1, x_up).start()
+    send(j_own, 3, x_dn).start()
+    send(j_own, 1, y_up).start()
+    send(j_own, 3, y_dn).start()
+    send(j_own, 2, x_up).start()
+    send(j_own, 0, x_dn).start()
+    send(j_own, 3, x_up).start()
+    send(j_own, 1, x_dn).start()
+
+    lane32 = lax.broadcasted_iota(jnp.int32, (32, LANES), 1)
+    left32 = lane32 < HALF
+
+    CHUNK = 128
+    last = nz // 2 - 1
+    ways = (True, False)
+    turns = [(c, k, up) for c in (1, 0) for k in range(3) for up in ways]
+
+    def goes(step, up, c):
+        return step < last or (step == last and c == (0 if up else 1))
+
+    def z_copy(s, step, up, c, k):
+        sems, recvs = (zp_send, zp_recv) if up else (zm_send, zm_recv)
+        ref = slabs.at[c, s, pl.ds(k * CHUNK, CHUNK), :]
+        return pltpu.make_async_remote_copy(
             src_ref=ref,
             dst_ref=ref,
-            send_sem=wa_send.at[d],
-            recv_sem=wa_recv.at[d],
+            send_sem=sems.at[step * 6 + c * 3 + k],
+            recv_sem=recvs.at[step * 6 + c * 3 + k],
+            device_id=z_up if up else z_dn,
+            device_id_type=MESH,
+        )
+
+    def z_out(step, up, c, k):
+        return z_copy((z + nz - step) % nz if up else (z + step) % nz, step, up, c, k)
+
+    def z_in(step, up, c, k):
+        return z_copy(z_slab(step, up), step, up, c, k)
+
+    def z_slab(step, up):
+        return (z + 2 * nz - step - 1) % nz if up else (z + step + 1) % nz
+
+    def hand_over(s, n):
+        ref = slabs.at[0, s]
+        return pltpu.make_async_remote_copy(
+            src_ref=ref,
+            dst_ref=ref,
+            send_sem=sl_send.at[n],
+            recv_sem=sl_recv.at[n],
             device_id=sib,
             device_id_type=MESH,
-        ).wait_recv()
-
-    lane32 = lax.broadcasted_iota(jnp.int32, (32, LANES), 1)
-    left32 = lane32 < HALF
-
-    CHUNK = 128
-
-    def z_ref(s, k):
-        return slabs.at[s, pl.ds(k * CHUNK, CHUNK), :]
-
-    def z_copy(step, up, k):
-        s = (z + nz - step) % nz if up else (z + step) % nz
-        sems, recvs = (zp_send, zp_recv) if up else (zm_send, zm_recv)
-        return pltpu.make_async_remote_copy(
-            src_ref=z_ref(s, k),
-            dst_ref=z_ref(s, k),
-            send_sem=sems.at[step * 3 + k],
-            recv_sem=recvs.at[step * 3 + k],
-            device_id=z_up if up else z_dn,
-            device_id_type=MESH,
         )
 
-    n_up = nz // 2
-    n_dn = nz - 1 - n_up
-
-    def z_send(step, up, k):
-        if step < (n_up if up else n_dn):
-            copy = z_copy(step, up, k)
-            copy.start()
-            sent.append(copy)
-
-    def z_arrived(step, up, k):
-        s = (z + 2 * nz - step - 1) % nz if up else (z + step + 1) % nz
-        sems, recvs = (zp_send, zp_recv) if up else (zm_send, zm_recv)
-        pltpu.make_async_remote_copy(
-            src_ref=z_ref(s, k),
-            dst_ref=z_ref(s, k),
-            send_sem=sems.at[step * 3 + k],
-            recv_sem=recvs.at[step * 3 + k],
-            device_id=z_up if up else z_dn,
-            device_id_type=MESH,
-        ).wait_recv()
-        return s
-
-    def unpack(s):
+    def came(step):
+        if step < 0:
+            return [(z, 15)]
+        if step == last:
+            return [(z_slab(step, True), step * 2)]
+        return [(z_slab(step, up), step * 2 + (0 if up else 1)) for up in ways]
+
+    @pl.when(core == 1)
+    def _():
+        wa[1, q] = w_ref[:, :, w_lanes(q)]
+        for c in (1, 0):
+            for d in range(c, GROUP):
+                ref = wa.at[c, (q + 8 - d) % 8]
+                pltpu.make_async_remote_copy(
+                    src_ref=ref,
+                    dst_ref=ref,
+                    send_sem=wa_send.at[d],
+                    recv_sem=wa_recv.at[c * 8 + d],
+                    device_id=sib,
+                    device_id_type=MESH,
+                ).wait_recv()
+            for k in range(3):
+                for g in range(4):
+                    if k < 2:
+                        lo, hi = wa[c, k * 4 + g, 0], wa[c, k * 4 + g, 1]
+                    else:
+                        lo, hi = wa[c, g, 2], wa[c, g + 4, 2]
+                    rows = jnp.where(left32, pick(lo.astype(F32), left32), pick(hi.astype(F32), left32))
+                    slabs[c, z, k * CHUNK + g * 32 : k * CHUNK + (g + 1) * 32, :] = rows.astype(BF16)
+                z_out(0, True, c, k).start()
+                z_out(0, False, c, k).start()
+        hand_over(z, 15).start()
+
+    def unpack(s, n):
+        @pl.when(core == 0)
+        def _():
+            hand_over(s, n).wait_recv()
+
         at = pl.multiple_of(s * 256, 256)
-        wfull[pl.ds(at, 256), 0:LANES] = slabs[s, 0:256, :]
-        v = slabs[s, 256:384, :]
+        wfull[pl.ds(at, 256), 0:LANES] = slabs[core, s, 0:256, :]
+        v = slabs[core, s, 256:384, :]
         wfull[pl.ds(at, 128), LANES:] = v
         wfull[pl.ds(at + 128, 128), LANES:] = swap(v.astype(F32)).astype(BF16)
 
-    for k in range(3):
-        for g in range(4):
-            if k < 2:
-                n = k * 4 + g
-                rows = jnp.where(left32, pick(wa[n, 0].astype(F32), left32), pick(wa[n, 1].astype(F32), left32))
-            else:
-                rows = jnp.where(
-                    left32, pick(wa[g, 2].astype(F32), left32), pick(wa[g + 4, 2].astype(F32), left32)
-                )
-            slabs[z, k * CHUNK + g * 32 : k * CHUNK + (g + 1) * 32, :] = rows.astype(BF16)
-        z_send(0, True, k)
-        z_send(0, False, k)
-
-    def z_round(step):
-        got = []
-        for k in range(3):
-            for up, most in ((True, n_up), (False, n_dn)):
-                if step < most:
-                    s = z_arrived(step, up, k)
-                    z_send(step + 1, up, k)
-                    if k == 0:
-                        got.append(s)
-        return got
+    def unpacks(step):
+        return [functools.partial(unpack, s, n) for s, n in came(step)]
+
+    def z_round(step, tasks):
+        @pl.when(core == 1)
+        def _():
+            todo = list(tasks)
+            for c, k, up in turns:
+                if goes(step, up, c):
+                    z_in(step, up, c, k).wait_recv()
+                if goes(step + 1, up, c):
+                    z_out(step + 1, up, c, k).start()
+                if (c, k, up) == turns[-1]:
+                    for s, n in came(step):
+                        hand_over(s, n).start()
+                if todo:
+                    todo.pop(0)()
+            for task in todo:
+                task()
+
+        @pl.when(core == 0)
+        def _():
+            for task in tasks:
+                task()
 
     for copy in fetch[3:]:
         copy.wait()
@@ -343,7 +377,7 @@
     def constants(first):
         dec = pick(dec_ref[:, lanes_q], left16)
         amp = pick(res_ref[:, lanes_q], left16) * jnp.sqrt(2.0 * dec)
-        for s in range(first, first + 4):
+        for s in (first, first + 1):
             d8 = dec[s : s + 1, :] * ones8
             amp_s[s] = amp[s : s + 1, :] * ones8
             lam_s[s] = jnp.exp(-d8)
@@ -362,18 +396,32 @@
 
     left64 = lax.broadcasted_iota(jnp.int32, (HALF, LANES), 1) < HALF
 
-    def products(j, lo, hi):
+    def products(j, steps):
         acc = None
-        for d in range(lo, hi + 1):
+        for d in steps:
             at = pl.multiple_of(((z + nz + d) % nz) * 256, 256)
             term = jnp.dot(X[j, :, pl.ds(at, 256)], wfull[pl.ds(at, 256), :], preferred_element_type=F32)
             acc = term if acc is None else acc + term
         return acc
 
     def here(j):
-        if j is not j_own:
-            for piece in range(4):
-                arrive_sib(j, piece)
+        for piece in range(4):
+            arrive_sib(j, piece)
+
+    def add_products(j, steps, first):
+        if first and j is not j_own:
+            here(j)
+        acc = products(j, steps)
+        part[j] = acc if first else part[j] + acc
+
+    done = {}
+
+    def product_tasks(j, reach, each=3):
+        steps = sorted(range(-reach, reach + 1), key=abs)
+        done[id(j)] = steps
+        return [
+            functools.partial(add_products, j, steps[i : i + each], i == 0) for i in range(0, len(steps), each)
+        ]
 
     def finish(j, acc):
         t0a, t0b = acc[0:HALF, 0:LANES], acc[HALF:, 0:LANES]
@@ -403,59 +451,47 @@
         for j, piece, onward in units[u]:
             arrive(j, piece)
             for dev in onward:
-                send(j, piece, dev)
+                send(j, piece, dev).start()
             waiting.append((j, piece))
 
     def to_sibling():
-        for j, piece in waiting:
-            send(j, piece, sib)
+        tasks = [send(j, piece, sib).start for j, piece in waiting]
         waiting.clear()
-
-    norm(1 - core, 0)
-    norm(1 - core, 1)
-    unpack(z)
+        return tasks
+
+    def consts(*firsts):
+        return [functools.partial(constants, s) for s in firsts]
+
+    for piece in range(4):
+        norm(1 - core, piece)
     unit(0)
-    for r in range(8):
-        got = z_round(r)
-        to_sibling()
-        for s in got:
-            unpack(s)
-        if r == 0:
-            norm(1 - core, 2)
-            norm(1 - core, 3)
-            unit(1)
-        elif r == 1:
-            constants(0)
-            unit(2)
-        elif r == 2:
-            constants(4)
-            constants(8)
-        elif r == 3:
-            constants(12)
-            unit(3)
-        elif r == 4:
-            z_weights()
-            unit(4)
-        elif r == 5:
-            for j in (j_own, p_own):
-                here(j)
-                part[j] = products(j, -6, 6)
-            unit(5)
-        elif r == 6:
-            for j in (j_dn, j_up):
-                here(j)
-                part[j] = products(j, -7, 7)
-            unit(6)
-            to_sibling()
-            for j in (j_op, p_up, p_dn):
-                here(j)
-                part[j] = products(j, -7, 7)
-    for j in (j_own, p_own):
-        finish(j, part[j] + products(j, -8, -7) + products(j, 7, 7))
-    for j in (j_dn, j_up, j_op, p_up, p_dn):
-        finish(j, part[j] + products(j, -8, -8))
-    here(p_op)
-    finish(p_op, products(p_op, -8, 7))
+    z_round(0, to_sibling() + unpacks(-1) + consts(0, 2))
+    unit(1)
+    z_round(1, to_sibling() + unpacks(0) + consts(4, 6, 8))
+    unit(2)
+    z_round(2, to_sibling() + unpacks(1) + consts(10, 12, 14))
+    z_round(3, unpacks(2) + [z_weights])
+    unit(3)
+    z_round(4, to_sibling() + unpacks(3) + product_tasks(j_own, 4))
+    unit(4)
+    z_round(5, to_sibling() + unpacks(4) + product_tasks(p_own, 5))
+    unit(5)
+    z_round(6, to_sibling() + unpacks(5) + product_tasks(j_dn, 6) + product_tasks(j_up, 6))
+    unit(6)
+    for task in to_sibling():
+        task()
+    z_round(
+        7,
+        unpacks(6)
+        + product_tasks(j_op, 7)
+        + product_tasks(p_up, 7)
+        + product_tasks(p_dn, 7)
+        + product_tasks(p_op, 7),
+    )
+    for task in unpacks(7):
+        task()
+    for j in (j_own, p_own, j_dn, j_up, j_op, p_up, p_dn, p_op):
+        finish(j, part[j] + products(j, [d for d in range(-8, 8) if d not in done[id(j)]]))
 
     rim_copy = pltpu.make_async_remote_copy(
         src_ref=proj.at[:, 504:512, :],
@@ -554,6 +590,20 @@
     @pl.loop(1, GROUP)
     def _(d):
         wa_copy(d).wait_send()
+
+    @pl.when(core == 0)
+    def _():
+        wa_copy(0).wait_send()
+
+    @pl.when(core == 1)
+    def _():
+        for step in range(last + 1):
+            for c, k, up in turns:
+                if goes(step, up, c):
+                    z_out(step, up, c, k).wait_send()
+        for step in range(-1, last + 1):
+            for s, n in came(step):
+                hand_over(s, n).wait_send()
 
     for d in range(1, nz):
 
@@ -655,13 +705,14 @@
         scratch_shapes=[
             pltpu.VMEM((rows, width), BF16),
             pltpu.VMEM((1, width), F32),
+            pltpu.VMEM((3, 32, channels), BF16),
             pltpu.VMEM((3, 3, channels), F32),
             pltpu.VMEM((MODES, channels), F32),
             pltpu.VMEM((MODES, channels), F32),
             pltpu.VMEM((1, channels), F32),
             pltpu.VMEM((GROUP, ROWS, width), BF16),
-            pltpu.VMEM((GROUP, 3, 32, LANES), BF16),
-            pltpu.VMEM((nz, 384, LANES), BF16),
+            pltpu.VMEM((2, GROUP, 3, 32, LANES), BF16),
+            pltpu.VMEM((2, nz, 384, LANES), BF16),
             pltpu.VMEM((width, 2 * LANES), BF16),
             pltpu.VMEM((GROUP, ROWS, 2 * LANES), F32),
             pltpu.VMEM((3, GROUP * HALF, LANES), F32),
@@ -682,14 +733,16 @@
             pltpu.VMEM((GROUP, HALF, LANES), BF16),
             dma((8,)),
             dma((8,)),
-            dma((8,)),
+            dma((16,)),
             dma((64,)),
             dma((32,)),
             dma((32,)),
-            dma((24,)),
-            dma((24,)),
-            dma((24,)),
-            dma((24,)),
+            dma((48,)),
+            dma((48,)),
+            dma((48,)),
+            dma((48,)),
+            dma((16,)),
+            dma((16,)),
             dma((2,)),
             dma((16,)),
             dma((16,)),

time: 67.1 us -> 62.1 us (0.925)
  the two profiles are of different devices: /device:TPU:32 before, /device:TPU:48 now
where the time goes in v3:
time: 62.1 us; the launch traced here: 61.9 us
  Pallas kernels  60.3 us (97%)
  local copies, waits for them, and re-layouts  1.57 us (3%)
    pallas_call x1, Pallas kernels, local(): pl.pallas_call(functools.partial(kernel, nz), out_shape=jax.ShapeDtypeStr...  60.3 us
    unnamed x1, local copies, waits for them, and re-layouts  1.57 us

profile of v3, /device:TPU:48, one launch (start us, length us, event | category | flops | bytes accessed | tf_op | source)
XLA Modules:
  0.0 61.9 jit_solution(14308381169898643306)
XLA Ops:
  0.0 60.3 %hyena.1 = bf16[128,512]{1,0:T(8,128)(2,1)} custom-call(bf16[128,4096]{1,0:T(8,128)(2,1)} %tok_hbm.1, f32[1,4096]{1,0:T(1,128)} %bitcast.4, bf16[3,32,512]{2,1,0:T(8,128)(2,1)} %bitcast.3, f32[3,3,512]{2,1,0:T(4,128)} %taps_hbm.1, f32[16,512]{1,0:T(8,128)} %dec_hbm.1, f32[16,512]{1,0:T(8,128)} %res_hbm.1, f32[1,512]{1,0:T(1,128)} %bitcast.5), custom_call_target="tpu_custom_call" | custom-call | tf_op jit(solution)/shard_map/hyena/pallas_call | solution.py:700
  60.3 1.6 %copy.9 = bf16[128,512]{1,0:T(8,128)(2,1)} copy(bf16[128,512]{1,0:T(8,128)(2,1)} %hyena.1) | data formatting | bytes 262144

commit v4 on v3

--- a/solution.py
+++ b/solution.py
@@ -37,7 +37,7 @@
     res_ref,
     skip_ref,
     X,
-    wa,
+    wpack,
     slabs,
     wfull,
     part,
@@ -106,9 +106,9 @@
         return pl.ds(pl.multiple_of(half * HALF, HALF), HALF)
 
     pairs = (
+        (w_hbm, w_ref),
         (tok_hbm.at[half_rows(core), :], tok_ref.at[half_rows(core), :]),
         (gain_hbm, gain_ref),
-        (w_hbm, w_ref),
         (tok_hbm.at[half_rows(1 - core), :], tok_ref.at[half_rows(1 - core), :]),
         (dec_hbm, dec_ref),
         (res_hbm, res_ref),
@@ -119,9 +119,6 @@
     for copy in fetch:
         copy.start()
 
-    def w_lanes(chip):
-        return pl.ds(pl.multiple_of((chip // 2) * LANES, LANES), LANES)
-
     totals[...] = jnp.zeros_like(totals)
 
     barrier = pltpu.get_barrier_semaphore()
@@ -134,10 +131,8 @@
         greet((base + (q + d) % 8, ch))
         greet((base + (q + d) % 8, y_hi * 2 + (1 - core)))
 
-    @pl.loop(1, nz)
-    def _(d):
-        greet((((z + d) % nz) * 8 + q, ch))
-
+    greet(z_up)
+    greet(z_dn)
     greet(y_far)
     greet(sib)
 
@@ -170,19 +165,31 @@
         X[j_own, rows, :] = (v * lax.rsqrt(ms + 1e-06) * gain_ref[...]).astype(BF16)
 
     fetch[0].wait()
+    left32 = lax.broadcasted_iota(jnp.int32, (32, LANES), 1) < HALF
+    left16 = lax.broadcasted_iota(jnp.int32, (16, LANES), 1) < HALF
+    for t in range(GROUP // 2):
+        f0, f1, f2 = [w_ref[i, :, t * LANES : (t + 1) * LANES].astype(F32) for i in range(3)]
+        r0, r1, r2 = swap(f0), swap(f1), swap(f2)
+        wpack[2 * t, 0:32, :] = jnp.where(left32, f0, r1).astype(BF16)
+        wpack[2 * t, 32:48, :] = jnp.where(left16, f2[0:16], r2[16:32]).astype(BF16)
+        wpack[2 * t + 1, 0:32, :] = jnp.where(left32, r0, f1).astype(BF16)
+        wpack[2 * t + 1, 32:48, :] = jnp.where(left16, r2[0:16], f2[16:32]).astype(BF16)
     fetch[1].wait()
+    fetch[2].wait()
     norm(core, 0)
     norm(core, 2)
-    fetch[2].wait()
-    pl.semaphore_wait(barrier, 7 + 7 + (nz - 1) + 2)
+    pl.semaphore_wait(barrier, 7 + 7 + 2 + 2)
 
     sent = []
+
+    def w_rows(c, chip):
+        return slabs.at[c, z, pl.ds(pl.multiple_of(chip * 48, 16), 48), :]
 
     def wa_copy(d):
         to = (q + d) % 8
         return pltpu.make_async_remote_copy(
-            src_ref=w_ref.at[:, :, w_lanes(to)],
-            dst_ref=wa.at[core, q],
+            src_ref=wpack.at[to],
+            dst_ref=w_rows(core, q),
             send_sem=wa_send.at[d],
             recv_sem=wa_recv.at[core * 8 + d],
             device_id=(base + to, y_hi * 2 + 1),
@@ -254,9 +261,6 @@
     send(j_own, 3, x_up).start()
     send(j_own, 1, x_dn).start()
 
-    lane32 = lax.broadcasted_iota(jnp.int32, (32, LANES), 1)
-    left32 = lane32 < HALF
-
     CHUNK = 128
     last = nz // 2 - 1
     ways = (True, False)
@@ -306,10 +310,10 @@
 
     @pl.when(core == 1)
     def _():
-        wa[1, q] = w_ref[:, :, w_lanes(q)]
+        slabs[1, z, pl.ds(pl.multiple_of(q * 48, 16), 48), :] = wpack[q]
         for c in (1, 0):
             for d in range(c, GROUP):
-                ref = wa.at[c, (q + 8 - d) % 8]
+                ref = w_rows(c, (q + 8 - d) % 8)
                 pltpu.make_async_remote_copy(
                     src_ref=ref,
                     dst_ref=ref,
@@ -319,13 +323,6 @@
                     device_id_type=MESH,
                 ).wait_recv()
             for k in range(3):
-                for g in range(4):
-                    if k < 2:
-                        lo, hi = wa[c, k * 4 + g, 0], wa[c, k * 4 + g, 1]
-                    else:
-                        lo, hi = wa[c, g, 2], wa[c, g + 4, 2]
-                    rows = jnp.where(left32, pick(lo.astype(F32), left32), pick(hi.astype(F32), left32))
-                    slabs[c, z, k * CHUNK + g * 32 : k * CHUNK + (g + 1) * 32, :] = rows.astype(BF16)
                 z_out(0, True, c, k).start()
                 z_out(0, False, c, k).start()
         hand_over(z, 15).start()
@@ -336,10 +333,11 @@
             hand_over(s, n).wait_recv()
 
         at = pl.multiple_of(s * 256, 256)
-        wfull[pl.ds(at, 256), 0:LANES] = slabs[core, s, 0:256, :]
-        v = slabs[core, s, 256:384, :]
-        wfull[pl.ds(at, 128), LANES:] = v
-        wfull[pl.ds(at + 128, 128), LANES:] = swap(v.astype(F32)).astype(BF16)
+        for g in range(GROUP):
+            v = slabs[core, s, g * 48 + 32 : g * 48 + 48, :]
+            wfull[pl.ds(at + g * 32, 32), 0:LANES] = slabs[core, s, g * 48 : g * 48 + 32, :]
+            wfull[pl.ds(at + g * 32, 16), LANES:] = v
+            wfull[pl.ds(at + g * 32 + 16, 16), LANES:] = swap(v.astype(F32)).astype(BF16)
 
     def unpacks(step):
         return [functools.partial(unpack, s, n) for s, n in came(step)]
@@ -369,8 +367,6 @@
     for copy in fetch[3:]:
         copy.wait()
     lanes_q = pl.ds(pl.multiple_of(tile * LANES, LANES), LANES)
-    lane16 = lax.broadcasted_iota(jnp.int32, (MODES, LANES), 1)
-    left16 = lane16 < HALF
     ones8 = jnp.ones((8, LANES), F32)
     subf = sub.astype(F32)
 
@@ -459,6 +455,11 @@
         waiting.clear()
         return tasks
 
+    def more(reach, *blocks):
+        for j in blocks:
+            done[id(j)] = done[id(j)] + [reach, -reach]
+        return [functools.partial(add_products, j, [reach, -reach], False) for j in blocks]
+
     def consts(*firsts):
         return [functools.partial(constants, s) for s in firsts]
 
@@ -474,15 +475,16 @@
     unit(3)
     z_round(4, to_sibling() + unpacks(3) + product_tasks(j_own, 4))
     unit(4)
-    z_round(5, to_sibling() + unpacks(4) + product_tasks(p_own, 5))
+    z_round(5, to_sibling() + unpacks(4) + more(5, j_own) + product_tasks(p_own, 5))
     unit(5)
-    z_round(6, to_sibling() + unpacks(5) + product_tasks(j_dn, 6) + product_tasks(j_up, 6))
+    z_round(6, to_sibling() + unpacks(5) + more(6, j_own, p_own) + product_tasks(j_dn, 6) + product_tasks(j_up, 6))
     unit(6)
     for task in to_sibling():
         task()
     z_round(
         7,
         unpacks(6)
+        + more(7, j_own, p_own, j_dn, j_up)
         + product_tasks(j_op, 7)
         + product_tasks(p_up, 7)
         + product_tasks(p_dn, 7)
@@ -711,7 +713,7 @@
             pltpu.VMEM((MODES, channels), F32),
             pltpu.VMEM((1, channels), F32),
             pltpu.VMEM((GROUP, ROWS, width), BF16),
-            pltpu.VMEM((2, GROUP, 3, 32, LANES), BF16),
+            pltpu.VMEM((GROUP, 48, LANES), BF16),
             pltpu.VMEM((2, nz, 384, LANES), BF16),
             pltpu.VMEM((width, 2 * LANES), BF16),
             pltpu.VMEM((GROUP, ROWS, 2 * LANES), F32),

time: 62.1 us -> 58.9 us (0.948)
  Pallas kernels: 60.3 us -> 57.2 us
    pallas_call x1, Pallas kernels: 60.3 us -> 57.2 us  [local(): pl.pallas_call(functools.partial(kernel, nz), out_shape=jax.ShapeDtypeStr...]
where the time goes in v4:
time: 58.9 us; the launch traced here: 58.7 us
  Pallas kernels  57.2 us (97%)
  local copies, waits for them, and re-layouts  1.57 us (3%)
    pallas_call x1, Pallas kernels, local(): pl.pallas_call(functools.partial(kernel, nz), out_shape=jax.ShapeDtypeStr...  57.2 us
    unnamed x1, local copies, waits for them, and re-layouts  1.57 us

profile of v4, /device:TPU:48, one launch (start us, length us, event | category | flops | bytes accessed | tf_op | source)
XLA Modules:
  0.0 58.7 jit_solution(3198261015781250478)
XLA Ops:
  0.0 57.2 %hyena.1 = bf16[128,512]{1,0:T(8,128)(2,1)} custom-call(bf16[128,4096]{1,0:T(8,128)(2,1)} %tok_hbm.1, f32[1,4096]{1,0:T(1,128)} %bitcast.4, bf16[3,32,512]{2,1,0:T(8,128)(2,1)} %bitcast.3, f32[3,3,512]{2,1,0:T(4,128)} %taps_hbm.1, f32[16,512]{1,0:T(8,128)} %dec_hbm.1, f32[16,512]{1,0:T(8,128)} %res_hbm.1, f32[1,512]{1,0:T(1,128)} %bitcast.5), custom_call_target="tpu_custom_call" | custom-call | tf_op jit(solution)/shard_map/hyena/pallas_call | solution.py:702
  57.2 1.6 %copy.9 = bf16[128,512]{1,0:T(8,128)(2,1)} copy(bf16[128,512]{1,0:T(8,128)(2,1)} %hyena.1) | data formatting | bytes 262144

commit v5 on v4

--- a/solution.py
+++ b/solution.py
@@ -126,14 +126,22 @@
     def greet(dev):
         pl.semaphore_signal(barrier, inc=1, device_id=dev, device_id_type=MESH)
 
-    @pl.loop(1, GROUP)
-    def _(d):
-        greet((base + (q + d) % 8, ch))
-        greet((base + (q + d) % 8, y_hi * 2 + (1 - core)))
-
-    greet(z_up)
-    greet(z_dn)
-    greet(y_far)
+    @pl.when(core == 1)
+    def _():
+        @pl.loop(1, GROUP)
+        def _(d):
+            greet((base + (q + d) % 8, ch))
+            greet((base + (q + d) % 8, y_hi * 2))
+
+        greet(z_up)
+        greet(z_dn)
+        greet(y_far)
+
+    @pl.when(core == 0)
+    def _():
+        for dev in (x_up, x_dn, y_up, y_dn):
+            greet(dev)
+
     greet(sib)
 
     lane = lax.broadcasted_iota(jnp.int32, (8, LANES), 1)
@@ -178,7 +186,7 @@
     fetch[2].wait()
     norm(core, 0)
     norm(core, 2)
-    pl.semaphore_wait(barrier, 7 + 7 + 2 + 2)
+    pl.semaphore_wait(barrier, 12 - core)
 
     sent = []
 
@@ -277,9 +285,12 @@
             dst_ref=ref,
             send_sem=sems.at[step * 6 + c * 3 + k],
             recv_sem=recvs.at[step * 6 + c * 3 + k],
-            device_id=z_up if up else z_dn,
+            device_id=(z_up[0], y_hi * 2) if straight(step, up, c) else z_up if up else z_dn,
             device_id_type=MESH,
         )
+
+    def straight(step, up, c):
+        return step == last and up and c == 0
 
     def z_out(step, up, c, k):
         return z_copy((z + nz - step) % nz if up else (z + step) % nz, step, up, c, k)
@@ -330,7 +341,11 @@
     def unpack(s, n):
         @pl.when(core == 0)
         def _():
-            hand_over(s, n).wait_recv()
+            if n == 2 * last:
+                for k in range(3):
+                    z_in(last, True, 0, k).wait_recv()
+            else:
+                hand_over(s, n).wait_recv()
 
         at = pl.multiple_of(s * 256, 256)
         for g in range(GROUP):
@@ -347,11 +362,11 @@
         def _():
             todo = list(tasks)
             for c, k, up in turns:
-                if goes(step, up, c):
+                if goes(step, up, c) and not straight(step, up, c):
                     z_in(step, up, c, k).wait_recv()
                 if goes(step + 1, up, c):
                     z_out(step + 1, up, c, k).start()
-                if (c, k, up) == turns[-1]:
+                if (c, k, up) == turns[-1] and step < last:
                     for s, n in came(step):
                         hand_over(s, n).start()
                 if todo:
@@ -410,11 +425,8 @@
         acc = products(j, steps)
         part[j] = acc if first else part[j] + acc
 
-    done = {}
-
     def product_tasks(j, reach, each=3):
         steps = sorted(range(-reach, reach + 1), key=abs)
-        done[id(j)] = steps
         return [
             functools.partial(add_products, j, steps[i : i + each], i == 0) for i in range(0, len(steps), each)
         ]
@@ -456,8 +468,6 @@
         return tasks
 
     def more(reach, *blocks):
-        for j in blocks:
-            done[id(j)] = done[id(j)] + [reach, -reach]
         return [functools.partial(add_products, j, [reach, -reach], False) for j in blocks]
 
     def consts(*firsts):
@@ -492,8 +502,7 @@
     )
     for task in unpacks(7):
         task()
-    for j in (j_own, p_own, j_dn, j_up, j_op, p_up, p_dn, p_op):
-        finish(j, part[j] + products(j, [d for d in range(-8, 8) if d not in done[id(j)]]))
+    finish(7, part[7] + products(7, (-8,)))
 
     rim_copy = pltpu.make_async_remote_copy(
         src_ref=proj.at[:, 504:512, :],
@@ -504,6 +513,8 @@
         device_id_type=MESH,
     )
     rim_copy.start()
+    for j in range(7):
+        finish(j, part[j] + products(j, (-8,)))
 
     def at_step(i, r):
         return proj[i, pl.ds(r, 8, stride=HALF), :]
@@ -534,7 +545,7 @@
         [before(i, 2, 0.0) for i in range(3)],
         [jnp.zeros((8, LANES), F32)] * MODES,
     )
-    ends = lax.fori_loop(0, HALF, scan_one, start, unroll=2)[2]
+    ends = lax.fori_loop(0, HALF, scan_one, start, unroll=4)[2]
 
     rim_copy.wait_recv()
 
@@ -603,7 +614,7 @@
             for c, k, up in turns:
                 if goes(step, up, c):
                     z_out(step, up, c, k).wait_send()
-        for step in range(-1, last + 1):
+        for step in range(-1, last):
             for s, n in came(step):
                 hand_over(s, n).wait_send()
 
@@ -643,7 +654,7 @@
         obuf[pl.ds(pl.multiple_of(r * 8, 8), 8), :] = gate_s[r] * (terms[0] + skp * drive)
         return states
 
-    lax.fori_loop(0, HALF, scan_two, states, unroll=2)
+    lax.fori_loop(0, HALF, scan_two, states, unroll=4)
 
     for j in range(GROUP):
         outbuf[j] = obuf[pl.ds(j, HALF, stride=8), :].astype(BF16)

time: 58.9 us -> 58 us (0.985)
  the two profiles are of different devices: /device:TPU:48 before, /device:TPU:40 now
where the time goes in v5:
time: 58 us; the launch traced here: 57.8 us
  Pallas kernels  56.3 us (97%)
  local copies, waits for them, and re-layouts  1.57 us (3%)
    pallas_call x1, Pallas kernels, local(): pl.pallas_call(functools.partial(kernel, nz), out_shape=jax.ShapeDtypeStr...  56.3 us
    unnamed x1, local copies, waits for them, and re-layouts  1.57 us

profile of v5, /device:TPU:40, one launch (start us, length us, event | category | flops | bytes accessed | tf_op | source)
XLA Modules:
  0.0 57.8 jit_solution(10655230592559040656)
XLA Ops:
  0.0 56.3 %hyena.1 = bf16[128,512]{1,0:T(8,128)(2,1)} custom-call(bf16[128,4096]{1,0:T(8,128)(2,1)} %tok_hbm.1, f32[1,4096]{1,0:T(1,128)} %bitcast.4, bf16[3,32,512]{2,1,0:T(8,128)(2,1)} %bitcast.3, f32[3,3,512]{2,1,0:T(4,128)} %taps_hbm.1, f32[16,512]{1,0:T(8,128)} %dec_hbm.1, f32[16,512]{1,0:T(8,128)} %res_hbm.1, f32[1,512]{1,0:T(1,128)} %bitcast.5), custom_call_target="tpu_custom_call" | custom-call | tf_op jit(solution)/shard_map/hyena/pallas_call | solution.py:713
  56.3 1.6 %copy.9 = bf16[128,512]{1,0:T(8,128)(2,1)} copy(bf16[128,512]{1,0:T(8,128)(2,1)} %hyena.1) | data formatting | bytes 262144

commit v6 on v5

--- a/solution.py
+++ b/solution.py
@@ -481,10 +481,10 @@
     z_round(1, to_sibling() + unpacks(0) + consts(4, 6, 8))
     unit(2)
     z_round(2, to_sibling() + unpacks(1) + consts(10, 12, 14))
-    z_round(3, unpacks(2) + [z_weights])
     unit(3)
+    z_round(3, to_sibling() + unpacks(2) + [z_weights])
+    unit(4)
     z_round(4, to_sibling() + unpacks(3) + product_tasks(j_own, 4))
-    unit(4)
     z_round(5, to_sibling() + unpacks(4) + more(5, j_own) + product_tasks(p_own, 5))
     unit(5)
     z_round(6, to_sibling() + unpacks(5) + more(6, j_own, p_own) + product_tasks(j_dn, 6) + product_tasks(j_up, 6))

time: 58 us -> 57.8 us (level)
  the two profiles are of different devices: /device:TPU:40 before, /device:TPU:48 now
where the time goes in v6:
time: 57.8 us; the launch traced here: 57.6 us
  Pallas kernels  56 us (97%)
  local copies, waits for them, and re-layouts  1.57 us (3%)
    pallas_call x1, Pallas kernels, local(): pl.pallas_call(functools.partial(kernel, nz), out_shape=jax.ShapeDtypeStr...  56 us
    unnamed x1, local copies, waits for them, and re-layouts  1.57 us

profile of v6, /device:TPU:48, one launch (start us, length us, event | category | flops | bytes accessed | tf_op | source)
XLA Modules:
  0.0 57.6 jit_solution(483187661122876651)
XLA Ops:
  0.0 56.0 %hyena.1 = bf16[128,512]{1,0:T(8,128)(2,1)} custom-call(bf16[128,4096]{1,0:T(8,128)(2,1)} %tok_hbm.1, f32[1,4096]{1,0:T(1,128)} %bitcast.4, bf16[3,32,512]{2,1,0:T(8,128)(2,1)} %bitcast.3, f32[3,3,512]{2,1,0:T(4,128)} %taps_hbm.1, f32[16,512]{1,0:T(8,128)} %dec_hbm.1, f32[16,512]{1,0:T(8,128)} %res_hbm.1, f32[1,512]{1,0:T(1,128)} %bitcast.5), custom_call_target="tpu_custom_call" | custom-call | tf_op jit(solution)/shard_map/hyena/pallas_call | solution.py:713
  56.0 1.6 %copy.9 = bf16[128,512]{1,0:T(8,128)(2,1)} copy(bf16[128,512]{1,0:T(8,128)(2,1)} %hyena.1) | data formatting | bytes 262144

commit v7 on v6

--- a/solution.py
+++ b/solution.py
@@ -656,9 +656,6 @@
 
     lax.fori_loop(0, HALF, scan_two, states, unroll=4)
 
-    for j in range(GROUP):
-        outbuf[j] = obuf[pl.ds(j, HALF, stride=8), :].astype(BF16)
-
     def out_copy(d):
         to = (q + d) % 8
         return pltpu.make_async_remote_copy(
@@ -671,9 +668,11 @@
         )
 
     for d in (6, 2, 7, 5, 3, 1, 4):
+        to = (q + d) % 8
+        outbuf[to] = obuf[pl.ds(to, HALF, stride=8), :].astype(BF16)
         out_copy(d).start()
 
-    inbox[q] = outbuf[q]
+    inbox[q] = obuf[pl.ds(q, HALF, stride=8), :].astype(BF16)
 
     for d in range(1, nz):
 

time: 57.8 us -> 57.8 us (level)
  no operation moved by 1% of the time
where the time goes in v7:
time: 57.8 us; the launch traced here: 57.6 us
  Pallas kernels  56 us (97%)
  local copies, waits for them, and re-layouts  1.57 us (3%)
    pallas_call x1, Pallas kernels, local(): pl.pallas_call(functools.partial(kernel, nz), out_shape=jax.ShapeDtypeStr...  56 us
    unnamed x1, local copies, waits for them, and re-layouts  1.57 us

profile of v7, /device:TPU:48, one launch (start us, length us, event | category | flops | bytes accessed | tf_op | source)
XLA Modules:
  0.0 57.6 jit_solution(18389367161413165938)
XLA Ops:
  0.0 56.0 %hyena.1 = bf16[128,512]{1,0:T(8,128)(2,1)} custom-call(bf16[128,4096]{1,0:T(8,128)(2,1)} %tok_hbm.1, f32[1,4096]{1,0:T(1,128)} %bitcast.4, bf16[3,32,512]{2,1,0:T(8,128)(2,1)} %bitcast.3, f32[3,3,512]{2,1,0:T(4,128)} %taps_hbm.1, f32[16,512]{1,0:T(8,128)} %dec_hbm.1, f32[16,512]{1,0:T(8,128)} %res_hbm.1, f32[1,512]{1,0:T(1,128)} %bitcast.5), custom_call_target="tpu_custom_call" | custom-call | tf_op jit(solution)/shard_map/hyena/pallas_call | solution.py:712
  56.0 1.6 %copy.9 = bf16[128,512]{1,0:T(8,128)(2,1)} copy(bf16[128,512]{1,0:T(8,128)(2,1)} %hyena.1) | data formatting | bytes 262144
